TPU v7x, 1024 devices: a whole 4x8x16 slice. The times are simulated.
1024 devices in a mesh: ty: 16 (over y, core), tx: 32 (over x_lo, z), grp: 2 (over x_hi).
Axes of the slice: x: 4 (x_hi: 2, x_lo: 2; x = x_hi * 2 + x_lo), y: 8, z: 16, core: 2. Of those that a mesh axis runs over, the one named last changes fastest.
Arguments:
- innovation: float32 [2, 131072, 2, 128], P(None, ('ty', 'tx', 'grp')), may hold values from -6 to 6
- obs_weight: float32 [2, 131072, 128], P(None, ('ty', 'tx', 'grp')), may hold values from 0.2 to 1
- depth_level: int32 [2, 131072, 128], P(None, ('ty', 'tx', 'grp')), may hold values from 0 to 7
- target_tile: int32 [2, 131072, 1], P(None, ('ty', 'tx', 'grp')), may hold values from 0 to 31; in each aligned block of 128 rows (0 to 127, 128 to 255, ..., all dimensions but the last counted through in order) at most 16 rows name the same one
- target_cell: int32 [2, 131072], P(None, ('ty', 'tx', 'grp')), may hold values from 0 to 1023
- land_sea: int32 [128, 8192], P('ty', ('tx', 'grp')), may hold values from 0 to 1, as said below
- horiz_diff: float32 [128, 8192], P('ty', ('tx', 'grp')), may hold values from 0.05 to 0.2
- vert_diff: float32 [8, 128, 8192], P(None, 'ty', ('tx', 'grp')), may hold values from 0.01 to 0.1
- coupling: float32 [5, 5], replicated, may hold values from -0.4 to 0.4
- ice_sensitivity: float32 [2, 4, 128, 8192], P(None, None, ('ty', 'grp'), 'tx'), may hold values from -6 to 6
Outputs:
- adjoint_state: float32 [5, 8, 128, 8192], P(None, None, 'ty', ('tx', 'grp'))
Inputs may be any that keep to these rules, and one draw needn't show every extreme that they name: `target_tile`: the rows of one device in one window name one tile column at most 16 times, and some device names one exactly 16 times. `target_cell`: cell index within the tile, row-major over 8 x 128. `land_sea`: 1 marks ocean, 0 land; the first and last grid rows are land.
All inputs are finite; a program needn't handle non-finite values.
Results may differ from a plain program's by a relative error of at most 0.00013.
Values sent between devices are 32-bit elements; how exact they have to be, the bound alone decides.
A program may use at most 32 MiB of HBM per device.

v0:
```python
import jax
import jax.numpy as jnp
from jax import lax
from jax.sharding import PartitionSpec as P

VARS = 2
ICEV = 4
ITERS = 2
SUB = 2


EXACT_DOT = lax.Precision.HIGHEST


def extended(block, sides, width):
    for axis, dim in sides:
        count = lax.axis_size(axis)
        forward = [(i, i + 1) for i in range(count - 1)]
        forward.append((count - 1, 0))
        backward = [(target, source) for source, target in forward]
        low = lax.ppermute(
            lax.slice_in_dim(block, block.shape[dim] - width, None, axis=dim), axis, forward
        )
        high = lax.ppermute(lax.slice_in_dim(block, 0, width, axis=dim), axis, backward)
        block = jnp.concatenate([low, block, high], axis=dim)
    return block


def advance(state_pad, diff_pad, ocean_pad, vertical_mid, ocean_mid, coupling, fields):
    center = state_pad[:, 1:-1, 1:-1]
    diff_center = diff_pad[1:-1, 1:-1]
    ocean_center = ocean_pad[1:-1, 1:-1]
    height = center.shape[1]
    width = center.shape[2]
    lateral = jnp.zeros_like(center)
    for y_start, x_start in ((2, 1), (0, 1), (1, 2), (1, 0)):
        near_state = state_pad[:, y_start : y_start + height, x_start : x_start + width]
        near_diff = diff_pad[y_start : y_start + height, x_start : x_start + width]
        near_ocean = ocean_pad[y_start : y_start + height, x_start : x_start + width]
        weight = 0.5 * (diff_center + near_diff) * ocean_center * near_ocean
        lateral = lateral + weight * (near_state - center)
    current = center.reshape(fields, -1, height, width)
    lateral = lateral.reshape(current.shape)
    upper = vertical_mid[:-1] * (current[:, 1:] - current[:, :-1])
    bottom = -vertical_mid[-1:] * current[:, -1:]
    vertical_flux = jnp.concatenate([upper, bottom], axis=1)
    below = jnp.concatenate([jnp.zeros_like(vertical_flux[:, :1]), vertical_flux[:, :-1]], axis=1)
    diffused = current + lateral + (vertical_flux - below)
    coupled = diffused + jnp.einsum("gf,glyx->flyx", coupling, diffused, precision=EXACT_DOT)
    return ocean_mid * coupled


def level_columns(innovation_w, weight_w, level_w, levels_count):
    level_ids = jnp.arange(levels_count, dtype=jnp.int32)
    onehot = (level_w[:, None, :] == level_ids[None, :, None]).astype(jnp.float32)
    weighted = weight_w[:, None, :] * innovation_w
    columns = jnp.einsum("pvk,plk->vlp", weighted, onehot, precision=EXACT_DOT)
    return columns.reshape(-1, innovation_w.shape[0])


def per_device(
    innovation,
    obs_weight,
    depth_level,
    target_tile,
    target_cell,
    land_sea,
    horiz_diff,
    vert_diff,
    coupling,
    ice_sensitivity,
):
    fields = coupling.shape[0]
    levels_count = vert_diff.shape[0]
    tile_rows = land_sea.shape[0]
    tile_cols = land_sea.shape[1]
    rows_here = innovation.shape[1]
    ocean_mask = land_sea.astype(jnp.float32)
    ice_tiles = lax.all_to_all(ice_sensitivity, "grp", split_axis=3, concat_axis=2, tiled=True)
    current = jnp.zeros((fields, levels_count, tile_rows, tile_cols), jnp.float32)
    state_rows = fields * levels_count
    for window in range(ITERS):
        columns = level_columns(
            innovation[window], obs_weight[window], depth_level[window], levels_count
        )
        dest_ids = target_tile[window][:, 0]
        cell_here = target_cell[window]
        empty_grid = jnp.zeros((columns.shape[0], tile_rows * tile_cols), jnp.float32)
        n_columns = lax.axis_size("tx")
        capacity = 4 * rows_here // n_columns
        dest_onehot = (dest_ids[:, None] == jnp.arange(n_columns, dtype=jnp.int32)[None, :]).astype(
            jnp.int32
        )
        earlier = jnp.cumsum(dest_onehot, axis=0) - dest_onehot
        rank_within = jnp.sum(earlier * dest_onehot, axis=1)
        slot_ids = dest_ids * capacity + rank_within
        payload = (
            jnp.zeros((columns.shape[0], n_columns * capacity), jnp.float32)
            .at[:, slot_ids]
            .set(columns)
        )
        cell_slots = (
            jnp.zeros((1, n_columns * capacity), jnp.float32)
            .at[0, slot_ids]
            .set(cell_here.astype(jnp.float32))
        )
        got_payload, got_cells = (
            lax.all_to_all(payload, "tx", split_axis=1, concat_axis=1, tiled=True),
            lax.all_to_all(cell_slots, "tx", split_axis=1, concat_axis=1, tiled=True),
        )
        grid = empty_grid.at[:, got_cells[0].astype(jnp.int32)].add(got_payload)
        profile = grid.reshape(VARS, levels_count, tile_rows, tile_cols)
        forcing = jnp.zeros((fields, levels_count, tile_rows, tile_cols), jnp.float32)
        forcing = forcing.at[:VARS].add(profile)
        forcing = forcing.at[:ICEV, 0].add(ice_tiles[window])
        current = current + ocean_mask * forcing
        for substep in range(SUB):
            packed = jnp.concatenate(
                [
                    current.reshape(state_rows, tile_rows, tile_cols),
                    horiz_diff[None],
                    ocean_mask[None],
                ],
                axis=0,
            )
            padded = extended(packed, (("ty", 1), (("tx", "grp"), 2)), 1)
            current = advance(
                padded[:state_rows],
                padded[state_rows],
                padded[state_rows + 1],
                vert_diff,
                ocean_mask,
                coupling,
                fields,
            )
    return current


def solution(mesh):
    in_specs = (
        P(None, ("ty", "tx", "grp"), None, None),
        P(None, ("ty", "tx", "grp"), None),
        P(None, ("ty", "tx", "grp"), None),
        P(None, ("ty", "tx", "grp"), None),
        P(None, ("ty", "tx", "grp")),
        P("ty", ("tx", "grp")),
        P("ty", ("tx", "grp")),
        P(None, "ty", ("tx", "grp")),
        P(),
        P(None, None, ("ty", "grp"), "tx"),
    )
    out_specs = P(None, None, "ty", ("tx", "grp"))
    return jax.shard_map(
        per_device, mesh=mesh, in_specs=in_specs, out_specs=out_specs, check_vma=False
    )
```

profile of v0, /device:TPU:1, one launch (start us, length us, event | category | flops | bytes accessed | tf_op | source)
XLA Modules:
  0.0 209.9 jit_solution(12097698489448238533)
XLA Ops:
  4.4 20.6 %all-to-all-start = ((f32[1,32,16]{2,0,1:T(1,128)}), f32[1,32,16]{2,0,1:T(1,128)S(1)}, u32[]{:S(2)}, u32[]{:S(2)}) async-start(f32[1,32,16]{2,0,1:T(1,128)} %bitcast.5), calls=%async_computation | async-start | bytes 32768 | tf_op jit(solution)/shard_map/all_to_all | solution.py:109
  29.1 8.1 %all-to-all-done = f32[1,32,16]{2,0,1:T(1,128)S(1)} async-done(((f32[1,32,16]{2,0,1:T(1,128)}), f32[1,32,16]{2,0,1:T(1,128)S(1)}, u32[]{:S(2)}, u32[]{:S(2)}) %all-to-all-start) | async-done | bytes 2080 | tf_op jit(solution)/shard_map/all_to_all | solution.py:109
  37.2 4.5 %all-to-all-start.3 = ((f32[1,32,16]{2,0,1:T(1,128)}), f32[1,32,16]{2,0,1:T(1,128)S(1)}, u32[]{:S(2)}, u32[]{:S(2)}) async-start(f32[1,32,16]{2,0,1:T(1,128)} %bitcast.39), calls=%async_computation.3 | async-start | bytes 32768 | tf_op jit(solution)/shard_map/all_to_all | solution.py:109
  47.7 6.0 %all-to-all-done.3 = f32[1,32,16]{2,0,1:T(1,128)S(1)} async-done(((f32[1,32,16]{2,0,1:T(1,128)}), f32[1,32,16]{2,0,1:T(1,128)S(1)}, u32[]{:S(2)}, u32[]{:S(2)}) %all-to-all-start.3) | async-done | bytes 2080 | tf_op jit(solution)/shard_map/all_to_all | solution.py:109
  53.8 3.7 %all-to-all-start.2 = ((f32[2,1,4096]{2,1,0:T(1,128)}), f32[2,1,4096]{2,1,0:T(1,128)S(1)}, u32[]{:S(2)}, u32[]{:S(2)}) async-start(f32[2,1,4096]{2,1,0:T(1,128)} %reshape.423), calls=%async_computation.2 | async-start | bytes 65536 | tf_op jit(solution)/shard_map/all_to_all | solution.py:79
  57.8 4.0 %all-to-all-done.2 = f32[2,1,4096]{2,1,0:T(1,128)S(1)} async-done(((f32[2,1,4096]{2,1,0:T(1,128)}), f32[2,1,4096]{2,1,0:T(1,128)S(1)}, u32[]{:S(2)}, u32[]{:S(2)}) %all-to-all-start.2) | async-done | bytes 32800 | tf_op jit(solution)/shard_map/all_to_all | solution.py:79
  61.8 6.0 %all-to-all-start.1 = ((f32[32,1,256]{2,1,0:T(1,128)}), f32[32,1,256]{2,1,0:T(1,128)S(1)}, u32[]{:S(2)}, u32[]{:S(2)}) async-start(f32[32,1,256]{2,1,0:T(1,128)} %reshape.425), calls=%async_computation.1 | async-start | bytes 65536 | tf_op jit(solution)/shard_map/all_to_all | solution.py:108
  70.9 9.5 %all-to-all-done.1 = f32[32,1,256]{2,1,0:T(1,128)S(1)} async-done(((f32[32,1,256]{2,1,0:T(1,128)}), f32[32,1,256]{2,1,0:T(1,128)S(1)}, u32[]{:S(2)}, u32[]{:S(2)}) %all-to-all-start.1) | async-done | bytes 32800 | tf_op jit(solution)/shard_map/all_to_all | solution.py:108
  80.4 3.9 %all-to-all-start.4 = ((f32[32,1,256]{2,1,0:T(1,128)}), f32[32,1,256]{2,1,0:T(1,128)S(1)}, u32[]{:S(2)}, u32[]{:S(2)}) async-start(f32[32,1,256]{2,1,0:T(1,128)} %reshape.421), calls=%async_computation.4 | async-start | bytes 65536 | tf_op jit(solution)/shard_map/all_to_all | solution.py:108
  85.1 3.4 %scatter_custom_fusion.2 = f32[16,1024]{0,1:T(8,128)S(1)} fusion(s32[512]{0:T(512)S(1)} %bitcast.197, f32[512,16]{1,0:T(8,128)S(1)} %bitcast.189, f32[]{:T(128)} %constant.113.clone.1), kind=kCustom, calls=%fused_computation.131 | custom fusion | flops 8192 | bytes 65540 | tf_op jit(solution)/shard_map/scatter-add | solution.py:111
  89.6 5.8 %collective-permute-start = (f32[42,1,128]{2,1,0:T(1,128)S(1)}, f32[42,1,128]{2,1,0:T(1,128)S(1)}, u32[]{:S(2)}, u32[]{:S(2)}) collective-permute-start(f32[42,1,128]{2,1,0:T(1,128)S(1)} %get-tuple-element.75), channel_id=1, source_target_pairs={{0,64},{64,128},{128,192},{192,256},{256,320},{320,384},{384,448},... | collective-permute-start | bytes 64520 | tf_op jit(solution)/shard_map/ppermute | solution.py:21
  104.0 6.1 %collective-permute-start.3 = (f32[42,10,1]{2,1,0:T(8,128)S(1)}, f32[42,10,1]{2,1,0:T(8,128)S(1)}, u32[]{:S(2)}, u32[]{:S(2)}) collective-permute-start(f32[42,10,1]{2,1,0:T(8,128)S(1)} %get-tuple-element.67), channel_id=1, source_target_pairs={{1,0},{2,1},{3,2},{4,3},{5,4},{6,5},{7,6},{8,7},{9,8},{10,9},{11,1... | collective-permute-start | bytes 5048 | tf_op jit(solution)/shard_map/ppermute | solution.py:24
  110.1 4.8 %collective-permute-done.2 = f32[42,10,1]{2,1,0:T(8,128)S(1)} collective-permute-done((f32[42,10,1]{2,1,0:T(8,128)S(1)}, f32[42,10,1]{2,1,0:T(8,128)S(1)}, u32[]{:S(2)}, u32[]{:S(2)}) %collective-permute-start.2) | collective-permute-done | bytes 1712 | tf_op jit(solution)/shard_map/ppermute | solution.py:21
  114.9 4.2 %collective-permute-done.3 = f32[42,10,1]{2,1,0:T(8,128)S(1)} collective-permute-done((f32[42,10,1]{2,1,0:T(8,128)S(1)}, f32[42,10,1]{2,1,0:T(8,128)S(1)}, u32[]{:S(2)}, u32[]{:S(2)}) %collective-permute-start.3) | collective-permute-done | bytes 1712 | tf_op jit(solution)/shard_map/ppermute | solution.py:24
  120.6 6.6 %collective-permute-start.4 = (f32[42,1,128]{2,1,0:T(1,128)S(1)}, f32[42,1,128]{2,1,0:T(1,128)S(1)}, u32[]{:S(2)}, u32[]{:S(2)}) collective-permute-start(f32[42,1,128]{2,1,0:T(1,128)S(1)} %get-tuple-element.73), channel_id=1, source_target_pairs={{0,64},{64,128},{128,192},{192,256},{256,320},{320,384},{384,448},... | collective-permute-start | bytes 64520 | tf_op jit(solution)/shard_map/ppermute | solution.py:21
  133.6 5.7 %collective-permute-start.7 = (f32[42,10,1]{2,1,0:T(8,128)S(1)}, f32[42,10,1]{2,1,0:T(8,128)S(1)}, u32[]{:S(2)}, u32[]{:S(2)}) collective-permute-start(f32[42,10,1]{2,1,0:T(8,128)S(1)} %get-tuple-element.65), channel_id=1, source_target_pairs={{1,0},{2,1},{3,2},{4,3},{5,4},{6,5},{7,6},{8,7},{9,8},{10,9},{11,1... | collective-permute-start | bytes 5048 | tf_op jit(solution)/shard_map/ppermute | solution.py:24
  139.3 9.8 %collective-permute-done.6 = f32[42,10,1]{2,1,0:T(8,128)S(1)} collective-permute-done((f32[42,10,1]{2,1,0:T(8,128)S(1)}, f32[42,10,1]{2,1,0:T(8,128)S(1)}, u32[]{:S(2)}, u32[]{:S(2)}) %collective-permute-start.6) | collective-permute-done | bytes 1712 | tf_op jit(solution)/shard_map/ppermute | solution.py:21
  149.1 3.4 %collective-permute-done.7 = f32[42,10,1]{2,1,0:T(8,128)S(1)} collective-permute-done((f32[42,10,1]{2,1,0:T(8,128)S(1)}, f32[42,10,1]{2,1,0:T(8,128)S(1)}, u32[]{:S(2)}, u32[]{:S(2)}) %collective-permute-start.7) | collective-permute-done | bytes 1712 | tf_op jit(solution)/shard_map/ppermute | solution.py:24
  161.1 6.7 %collective-permute-start.11 = (f32[42,10,1]{2,1,0:T(8,128)S(1)}, f32[42,10,1]{2,1,0:T(8,128)S(1)}, u32[]{:S(2)}, u32[]{:S(2)}) collective-permute-start(f32[42,10,1]{2,1,0:T(8,128)S(1)} %get-tuple-element.63), channel_id=1, source_target_pairs={{1,0},{2,1},{3,2},{4,3},{5,4},{6,5},{7,6},{8,7},{9,8},{10,9},{11,1... | collective-permute-start | bytes 5048 | tf_op jit(solution)/shard_map/ppermute | solution.py:24
  167.8 9.2 %collective-permute-done.10 = f32[42,10,1]{2,1,0:T(8,128)S(1)} collective-permute-done((f32[42,10,1]{2,1,0:T(8,128)S(1)}, f32[42,10,1]{2,1,0:T(8,128)S(1)}, u32[]{:S(2)}, u32[]{:S(2)}) %collective-permute-start.10) | collective-permute-done | bytes 1712 | tf_op jit(solution)/shard_map/ppermute | solution.py:21
  177.0 3.6 %collective-permute-done.11 = f32[42,10,1]{2,1,0:T(8,128)S(1)} collective-permute-done((f32[42,10,1]{2,1,0:T(8,128)S(1)}, f32[42,10,1]{2,1,0:T(8,128)S(1)}, u32[]{:S(2)}, u32[]{:S(2)}) %collective-permute-start.11) | collective-permute-done | bytes 1712 | tf_op jit(solution)/shard_map/ppermute | solution.py:24
  188.9 6.7 %collective-permute-start.15 = (f32[42,10,1]{2,1,0:T(8,128)S(1)}, f32[42,10,1]{2,1,0:T(8,128)S(1)}, u32[]{:S(2)}, u32[]{:S(2)}) collective-permute-start(f32[42,10,1]{2,1,0:T(8,128)S(1)} %get-tuple-element.61), channel_id=1, source_target_pairs={{1,0},{2,1},{3,2},{4,3},{5,4},{6,5},{7,6},{8,7},{9,8},{10,9},{11,1... | collective-permute-start | bytes 5048 | tf_op jit(solution)/shard_map/ppermute | solution.py:24
  195.6 7.9 %collective-permute-done.14 = f32[42,10,1]{2,1,0:T(8,128)S(1)} collective-permute-done((f32[42,10,1]{2,1,0:T(8,128)S(1)}, f32[42,10,1]{2,1,0:T(8,128)S(1)}, u32[]{:S(2)}, u32[]{:S(2)}) %collective-permute-start.14) | collective-permute-done | bytes 1712 | tf_op jit(solution)/shard_map/ppermute | solution.py:21
  203.5 4.2 %collective-permute-done.15 = f32[42,10,1]{2,1,0:T(8,128)S(1)} collective-permute-done((f32[42,10,1]{2,1,0:T(8,128)S(1)}, f32[42,10,1]{2,1,0:T(8,128)S(1)}, u32[]{:S(2)}, u32[]{:S(2)}) %collective-permute-start.15) | collective-permute-done | bytes 1712 | tf_op jit(solution)/shard_map/ppermute | solution.py:24
  (144 shorter events, 54.9 us)
Async XLA Ops:
  0.0 119.9 %copy-start = (f32[5,5]{1,0:T(8,128)S(1)}, f32[5,5]{1,0:T(8,128)}, u32[]{:S(2)}) copy-start(f32[5,5]{1,0:T(8,128)} %param.26) | copy-start | bytes 304
  1.2 23.9 %copy-start.2 = (f32[2,128,128]{2,1,0:T(8,128)S(1)}, f32[2,128,128]{2,1,0:T(8,128)}, u32[]{:S(2)}) copy-start(f32[2,128,128]{2,1,0:T(8,128)} %param.19) | copy-start | bytes 393220
  4.4 32.7 %all-to-all-start = ((f32[1,32,16]{2,0,1:T(1,128)}), f32[1,32,16]{2,0,1:T(1,128)S(1)}, u32[]{:S(2)}, u32[]{:S(2)}) async-start(f32[1,32,16]{2,0,1:T(1,128)} %bitcast.5), calls=%async_computation | async-start | bytes 32768 | tf_op jit(solution)/shard_map/all_to_all | solution.py:109
  27.4 14.2 %copy-start.5 = (f32[8,8,128]{2,1,0:T(8,128)S(1)}, f32[8,8,128]{2,1,0:T(8,128)}, u32[]{:S(2)}) copy-start(f32[8,8,128]{2,1,0:T(8,128)} %param.25) | copy-start | bytes 98308
  37.2 16.6 %all-to-all-start.3 = ((f32[1,32,16]{2,0,1:T(1,128)}), f32[1,32,16]{2,0,1:T(1,128)S(1)}, u32[]{:S(2)}, u32[]{:S(2)}) async-start(f32[1,32,16]{2,0,1:T(1,128)} %bitcast.39), calls=%async_computation.3 | async-start | bytes 32768 | tf_op jit(solution)/shard_map/all_to_all | solution.py:109
  53.8 8.0 %all-to-all-start.2 = ((f32[2,1,4096]{2,1,0:T(1,128)}), f32[2,1,4096]{2,1,0:T(1,128)S(1)}, u32[]{:S(2)}, u32[]{:S(2)}) async-start(f32[2,1,4096]{2,1,0:T(1,128)} %reshape.423), calls=%async_computation.2 | async-start | bytes 65536 | tf_op jit(solution)/shard_map/all_to_all | solution.py:79
  61.8 18.6 %all-to-all-start.1 = ((f32[32,1,256]{2,1,0:T(1,128)}), f32[32,1,256]{2,1,0:T(1,128)S(1)}, u32[]{:S(2)}, u32[]{:S(2)}) async-start(f32[32,1,256]{2,1,0:T(1,128)} %reshape.425), calls=%async_computation.1 | async-start | bytes 65536 | tf_op jit(solution)/shard_map/all_to_all | solution.py:108
  80.4 16.4 %all-to-all-start.4 = ((f32[32,1,256]{2,1,0:T(1,128)}), f32[32,1,256]{2,1,0:T(1,128)S(1)}, u32[]{:S(2)}, u32[]{:S(2)}) async-start(f32[32,1,256]{2,1,0:T(1,128)} %reshape.421), calls=%async_computation.4 | async-start | bytes 65536 | tf_op jit(solution)/shard_map/all_to_all | solution.py:108
  89.6 11.6 %collective-permute-start = (f32[42,1,128]{2,1,0:T(1,128)S(1)}, f32[42,1,128]{2,1,0:T(1,128)S(1)}, u32[]{:S(2)}, u32[]{:S(2)}) collective-permute-start(f32[42,1,128]{2,1,0:T(1,128)S(1)} %get-tuple-element.75), channel_id=1, source_target_pairs={{0,64},{64,128},{128,192},{192,256},{256,320},{320,384},{384,448},... | collective-permute-start | bytes 64520 | tf_op jit(solution)/shard_map/ppermute | solution.py:21
  95.4 5.8 %collective-permute-start.1 = (f32[42,1,128]{2,1,0:T(1,128)S(1)}, f32[42,1,128]{2,1,0:T(1,128)S(1)}, u32[]{:S(2)}, u32[]{:S(2)}) collective-permute-start(f32[42,1,128]{2,1,0:T(1,128)S(1)} %get-tuple-element.76), channel_id=1, source_target_pairs={{64,0},{128,64},{192,128},{256,192},{320,256},{384,320},{448,384},... | collective-permute-start | bytes 64520 | tf_op jit(solution)/shard_map/ppermute | solution.py:24
  101.5 13.4 %collective-permute-start.2 = (f32[42,10,1]{2,1,0:T(8,128)S(1)}, f32[42,10,1]{2,1,0:T(8,128)S(1)}, u32[]{:S(2)}, u32[]{:S(2)}) collective-permute-start(f32[42,10,1]{2,1,0:T(8,128)S(1)} %get-tuple-element.68), channel_id=1, source_target_pairs={{0,1},{1,2},{2,3},{3,4},{4,5},{5,6},{6,7},{7,8},{8,9},{9,10},{10,1... | collective-permute-start | bytes 5048 | tf_op jit(solution)/shard_map/ppermute | solution.py:21
  104.0 15.1 %collective-permute-start.3 = (f32[42,10,1]{2,1,0:T(8,128)S(1)}, f32[42,10,1]{2,1,0:T(8,128)S(1)}, u32[]{:S(2)}, u32[]{:S(2)}) collective-permute-start(f32[42,10,1]{2,1,0:T(8,128)S(1)} %get-tuple-element.67), channel_id=1, source_target_pairs={{1,0},{2,1},{3,2},{4,3},{5,4},{6,5},{7,6},{8,7},{9,8},{10,9},{11,1... | collective-permute-start | bytes 5048 | tf_op jit(solution)/shard_map/ppermute | solution.py:24
  120.6 7.5 %collective-permute-start.4 = (f32[42,1,128]{2,1,0:T(1,128)S(1)}, f32[42,1,128]{2,1,0:T(1,128)S(1)}, u32[]{:S(2)}, u32[]{:S(2)}) collective-permute-start(f32[42,1,128]{2,1,0:T(1,128)S(1)} %get-tuple-element.73), channel_id=1, source_target_pairs={{0,64},{64,128},{128,192},{192,256},{256,320},{320,384},{384,448},... | collective-permute-start | bytes 64520 | tf_op jit(solution)/shard_map/ppermute | solution.py:21
  127.2 3.2 %collective-permute-start.5 = (f32[42,1,128]{2,1,0:T(1,128)S(1)}, f32[42,1,128]{2,1,0:T(1,128)S(1)}, u32[]{:S(2)}, u32[]{:S(2)}) collective-permute-start(f32[42,1,128]{2,1,0:T(1,128)S(1)} %get-tuple-element.74), channel_id=1, source_target_pairs={{64,0},{128,64},{192,128},{256,192},{320,256},{384,320},{448,384},... | collective-permute-start | bytes 64520 | tf_op jit(solution)/shard_map/ppermute | solution.py:24
  130.7 18.4 %collective-permute-start.6 = (f32[42,10,1]{2,1,0:T(8,128)S(1)}, f32[42,10,1]{2,1,0:T(8,128)S(1)}, u32[]{:S(2)}, u32[]{:S(2)}) collective-permute-start(f32[42,10,1]{2,1,0:T(8,128)S(1)} %get-tuple-element.66), channel_id=1, source_target_pairs={{0,1},{1,2},{2,3},{3,4},{4,5},{5,6},{6,7},{7,8},{8,9},{9,10},{10,1... | collective-permute-start | bytes 5048 | tf_op jit(solution)/shard_map/ppermute | solution.py:21
  133.6 18.9 %collective-permute-start.7 = (f32[42,10,1]{2,1,0:T(8,128)S(1)}, f32[42,10,1]{2,1,0:T(8,128)S(1)}, u32[]{:S(2)}, u32[]{:S(2)}) collective-permute-start(f32[42,10,1]{2,1,0:T(8,128)S(1)} %get-tuple-element.65), channel_id=1, source_target_pairs={{1,0},{2,1},{3,2},{4,3},{5,4},{6,5},{7,6},{8,7},{9,8},{10,9},{11,1... | collective-permute-start | bytes 5048 | tf_op jit(solution)/shard_map/ppermute | solution.py:24
  154.1 2.3 %collective-permute-start.8 = (f32[42,1,128]{2,1,0:T(1,128)S(1)}, f32[42,1,128]{2,1,0:T(1,128)S(1)}, u32[]{:S(2)}, u32[]{:S(2)}) collective-permute-start(f32[42,1,128]{2,1,0:T(1,128)S(1)} %get-tuple-element.71), channel_id=1, source_target_pairs={{0,64},{64,128},{128,192},{192,256},{256,320},{320,384},{384,448},... | collective-permute-start | bytes 64520 | tf_op jit(solution)/shard_map/ppermute | solution.py:21
  155.4 3.5 %collective-permute-start.9 = (f32[42,1,128]{2,1,0:T(1,128)S(1)}, f32[42,1,128]{2,1,0:T(1,128)S(1)}, u32[]{:S(2)}, u32[]{:S(2)}) collective-permute-start(f32[42,1,128]{2,1,0:T(1,128)S(1)} %get-tuple-element.72), channel_id=1, source_target_pairs={{64,0},{128,64},{192,128},{256,192},{320,256},{384,320},{448,384},... | collective-permute-start | bytes 64520 | tf_op jit(solution)/shard_map/ppermute | solution.py:24
  159.2 17.8 %collective-permute-start.10 = (f32[42,10,1]{2,1,0:T(8,128)S(1)}, f32[42,10,1]{2,1,0:T(8,128)S(1)}, u32[]{:S(2)}, u32[]{:S(2)}) collective-permute-start(f32[42,10,1]{2,1,0:T(8,128)S(1)} %get-tuple-element.64), channel_id=1, source_target_pairs={{0,1},{1,2},{2,3},{3,4},{4,5},{5,6},{6,7},{7,8},{8,9},{9,10},{10,1... | collective-permute-start | bytes 5048 | tf_op jit(solution)/shard_map/ppermute | solution.py:21
  161.1 19.5 %collective-permute-start.11 = (f32[42,10,1]{2,1,0:T(8,128)S(1)}, f32[42,10,1]{2,1,0:T(8,128)S(1)}, u32[]{:S(2)}, u32[]{:S(2)}) collective-permute-start(f32[42,10,1]{2,1,0:T(8,128)S(1)} %get-tuple-element.63), channel_id=1, source_target_pairs={{1,0},{2,1},{3,2},{4,3},{5,4},{6,5},{7,6},{8,7},{9,8},{10,9},{11,1... | collective-permute-start | bytes 5048 | tf_op jit(solution)/shard_map/ppermute | solution.py:24
  182.2 2.3 %collective-permute-start.12 = (f32[42,1,128]{2,1,0:T(1,128)S(1)}, f32[42,1,128]{2,1,0:T(1,128)S(1)}, u32[]{:S(2)}, u32[]{:S(2)}) collective-permute-start(f32[42,1,128]{2,1,0:T(1,128)S(1)} %get-tuple-element.69), channel_id=1, source_target_pairs={{0,64},{64,128},{128,192},{192,256},{256,320},{320,384},{384,448},... | collective-permute-start | bytes 64520 | tf_op jit(solution)/shard_map/ppermute | solution.py:21
  183.5 3.2 %collective-permute-start.13 = (f32[42,1,128]{2,1,0:T(1,128)S(1)}, f32[42,1,128]{2,1,0:T(1,128)S(1)}, u32[]{:S(2)}, u32[]{:S(2)}) collective-permute-start(f32[42,1,128]{2,1,0:T(1,128)S(1)} %get-tuple-element.70), channel_id=1, source_target_pairs={{64,0},{128,64},{192,128},{256,192},{320,256},{384,320},{448,384},... | collective-permute-start | bytes 64520 | tf_op jit(solution)/shard_map/ppermute | solution.py:24
  187.0 16.6 %collective-permute-start.14 = (f32[42,10,1]{2,1,0:T(8,128)S(1)}, f32[42,10,1]{2,1,0:T(8,128)S(1)}, u32[]{:S(2)}, u32[]{:S(2)}) collective-permute-start(f32[42,10,1]{2,1,0:T(8,128)S(1)} %get-tuple-element.62), channel_id=1, source_target_pairs={{0,1},{1,2},{2,3},{3,4},{4,5},{5,6},{6,7},{7,8},{8,9},{9,10},{10,1... | collective-permute-start | bytes 5048 | tf_op jit(solution)/shard_map/ppermute | solution.py:21
  188.9 18.9 %collective-permute-start.15 = (f32[42,10,1]{2,1,0:T(8,128)S(1)}, f32[42,10,1]{2,1,0:T(8,128)S(1)}, u32[]{:S(2)}, u32[]{:S(2)}) collective-permute-start(f32[42,10,1]{2,1,0:T(8,128)S(1)} %get-tuple-element.61), channel_id=1, source_target_pairs={{1,0},{2,1},{3,2},{4,3},{5,4},{6,5},{7,6},{8,7},{9,8},{10,9},{11,1... | collective-permute-start | bytes 5048 | tf_op jit(solution)/shard_map/ppermute | solution.py:24
  (7 other events, 5.4 us)
where the time goes:
time: 212 us; the launch traced here: 210 us
  starting transfers between devices  88.5 us (42%)
  waiting for transfers between devices  85.6 us (40%)
  local copies, waits for them, and re-layouts  17.9 us (8%)
  other arithmetic  13.8 us (7%)
  matrix products  3.43 us (2%)
    ppermute x8, waiting for transfers between devices, extended(): lax.ppermute(lax.slice_in_dim(block, block.shape[dim] - width, None, axis...  34.1 us
    ppermute x8, starting transfers between devices, extended(): lax.ppermute(lax.slice_in_dim(block, 0, width, axis=dim), axis, backward)  25.5 us
    all_to_all x2, starting transfers between devices, per_device(): lax.all_to_all(cell_slots, 'tx', split_axis=1, concat_axis=1, tiled=True)  25.1 us
    ppermute x8, starting transfers between devices, extended(): lax.ppermute(lax.slice_in_dim(block, block.shape[dim] - width, None, axis...  24.3 us
    ppermute x8, waiting for transfers between devices, extended(): lax.ppermute(lax.slice_in_dim(block, 0, width, axis=dim), axis, backward)  22.5 us
    all_to_all x2, waiting for transfers between devices, per_device(): lax.all_to_all(cell_slots, 'tx', split_axis=1, concat_axis=1, tiled=True)  14.1 us
    all_to_all x2, waiting for transfers between devices, per_device(): lax.all_to_all(payload, 'tx', split_axis=1, concat_axis=1, tiled=True)  10.8 us
    all_to_all x2, starting transfers between devices, per_device(): lax.all_to_all(payload, 'tx', split_axis=1, concat_axis=1, tiled=True)  9.89 us
  transfers between devices with their start and end apart: 21, of which 19 were waited for; matrix products, arithmetic and copies ran while one was open for 10% of the time, Pallas kernels for 0%

commit v1 on v0

v1 whole, which is shorter than its diff:
```python
import functools

import jax
import jax.numpy as jnp
from jax import lax
from jax.experimental import pallas as pl
from jax.experimental.pallas import tpu as pltpu
from jax.sharding import PartitionSpec as P

F = 5
LEV = 8
VARS = 2
ICEV = 4
ROWS = 8
LANES = 128
DEPTH = 128
PROFS = 128
ITERS = 2
SUB = 2
SLOTS = 32
N_FORCED = VARS * LEV + (ICEV - VARS)
N_STATIC = LEV + 2
MESH = pl.DeviceIdType.MESH
F32 = jnp.float32
BF16 = jnp.bfloat16
NT = (((1,), (1,)), ((), ()))

FORCED = [(f, l) for f in range(VARS) for l in range(LEV)] + [(f, 0) for f in range(VARS, ICEV)]

L_LEVEL, L_WEIGHT, L_INNOV = 0, 2, 4
L_TILE, L_CELL, L_LAND, L_HDIFF, L_VDIFF, L_ICE, L_OWN = 6, 7, 8, 9, 10, 11, 12
N_LOCAL = 14
R_ROUTE, R_ICE, R_STAT_Y, R_STAT_X, R_F_Y, R_F_X = 0, 2, 3, 4, 5, 7
N_REMOTE = 9


def iota(shape, axis):
    return lax.broadcasted_iota(jnp.int32, shape, axis)


def split(x):
    high = x.astype(BF16)
    low = (x - high.astype(F32)).astype(BF16)
    return high, low


def roll_lanes(x, shift):
    shift %= LANES
    return x if shift == 0 else pltpu.roll(x, shift, 1)


def dot_nt(a, b):
    return lax.dot_general(a, b, NT, preferred_element_type=F32)


def pack_messages(weight, level, innovs, tile, cell):
    level_t = level.T
    columns = []
    for innov in innovs:
        weighted_t = (weight * innov).T
        rows = [
            jnp.sum(jnp.where(level_t == l, weighted_t, 0.0), axis=0, keepdims=True) for l in range(LEV)
        ]
        columns.append(jnp.concatenate(rows, axis=0))
    named = tile == iota((SLOTS, PROFS), 0)
    named_f = named.astype(F32)
    named_b = named_f.astype(BF16)
    before = (iota((PROFS, PROFS), 0) < iota((PROFS, PROFS), 1)).astype(F32).astype(BF16)
    counts = lax.dot_general(named_b, before, (((1,), (0,)), ((), ())), preferred_element_type=F32)
    rank = jnp.sum(named_f * counts, axis=0, keepdims=True).astype(jnp.int32)
    cell_y = (cell // LANES).astype(F32)
    cell_x = (cell % LANES).astype(F32)
    high, low = [], []
    parts = []
    for column in columns:
        top = column.astype(BF16).astype(F32)
        parts.append((top, column - top))
    for upper in range(2):
        for top, rest in parts:
            for r in range(8):
                here = rank == upper * 8 + r
                high.append(jnp.where(here, top, 0.0))
                low.append(jnp.where(here, rest, 0.0))
    row = iota((8, PROFS), 0)
    zero = jnp.zeros((8, PROFS), F32)
    for r in range(8):
        first, second = rank == r, rank == r + 8
        block = jnp.where(jnp.logical_and(row == 0, first), cell_y, 0.0)
        block = jnp.where(jnp.logical_and(row == 1, first), cell_x, block)
        block = jnp.where(jnp.logical_and(row == 2, second), cell_y, block)
        block = jnp.where(jnp.logical_and(row == 3, second), cell_x, block)
        high.append(block)
        low.append(zero)
    high += [zero] * 8
    low += [zero] * 8
    values = jnp.concatenate(
        [jnp.concatenate(high, axis=0).astype(BF16), jnp.concatenate(low, axis=0).astype(BF16)], axis=1
    )
    return dot_nt(jnp.concatenate([named_b, named_b], axis=1), values)


def gather_cells(first, second, cells):
    got = jnp.concatenate([first, second, roll_lanes(first, -8), roll_lanes(second, -8)], axis=0).T
    where_ = jnp.concatenate(
        [cells, roll_lanes(cells, -2), roll_lanes(cells, -8), roll_lanes(cells, -10)], axis=0
    ).T
    top = got.astype(BF16).astype(F32)
    rest = got - top
    y_of_row = iota((ROWS, LANES), 0).astype(F32)
    x_of_row = iota((LANES, LANES), 0).astype(F32)
    left, right = [], []
    for r in range(0, 8, 2):
        y_here = where_[r * 8 : r * 8 + 1] == y_of_row
        x_here = (where_[r * 8 + 1 : r * 8 + 2] == x_of_row).astype(F32).astype(BF16)
        for part in (top, rest):
            blocks = []
            for v in range(VARS):
                for l in range(LEV):
                    at = v * 64 + r * 8 + l
                    blocks.append(jnp.where(y_here, part[at : at + 1], 0.0))
            left.append(jnp.concatenate(blocks, axis=0).astype(BF16))
            right.append(x_here)
    return dot_nt(jnp.concatenate(left, axis=1), jnp.concatenate(right, axis=1))


def pack_edges(items):
    lane = iota((ROWS, LANES), 1)
    last = jnp.zeros((ROWS, LANES), F32)
    first = jnp.zeros((ROWS, LANES), F32)
    for slot, level, rows in items:
        at = 16 * level + 4 * slot
        turned = roll_lanes(rows, at + 4)
        last = jnp.where(jnp.logical_and(lane >= at, lane < at + 4), turned, last)
        first = jnp.where(jnp.logical_and(lane >= at + 4, lane < at + 8), turned, first)
    return last, first


def strip(slot, from_left, own_last, own_first, from_right):
    group = iota((ROWS, LANES), 1) % 16
    low = jnp.where(group < 4, roll_lanes(from_left, -4 * slot), roll_lanes(own_first, -4 * slot))
    high = jnp.where(group < 12, roll_lanes(own_last, 8 - 4 * slot), roll_lanes(from_right, 8 - 4 * slot))
    return jnp.where(group < 8, low, high)


def strips(slots, received, own):
    upper = iota((ROWS, LANES), 0) < 4
    left_halo = jnp.where(upper, received[1], received[2])
    right_halo = jnp.where(upper, received[4], received[5])
    sides = ((received[0], received[3]), (left_halo, right_halo))
    return [
        tuple(strip(slot, sides[t][0], own[t][0], own[t][1], sides[t][1]) for t in range(2)) for slot in slots
    ]


def y_neighbours(pair):
    row = iota((ROWS, LANES), 0)
    a, b = pair
    next_a, next_b = pltpu.roll(a, ROWS - 1, 0), pltpu.roll(b, ROWS - 1, 0)
    prev_a, prev_b = pltpu.roll(a, 1, 0), pltpu.roll(b, 1, 0)
    plus = (jnp.where(row == ROWS - 1, next_b, next_a), jnp.where(row == ROWS - 1, next_a, next_b))
    minus = (jnp.where(row == 0, prev_b, prev_a), jnp.where(row == 0, prev_a, prev_b))
    return plus, minus


def edge_pair(one):
    group = iota((ROWS, LANES), 1) % 16
    return jnp.where(group == 13, roll_lanes(one, 10), one)


def x_neighbours(one, edges, level):
    lane = iota((ROWS, LANES), 1)
    halo = roll_lanes(edges, LANES - 1 - 12 - 16 * level)
    plus = jnp.where(lane == LANES - 1, halo, roll_lanes(one, -1))
    minus = jnp.where(lane == 0, halo, roll_lanes(one, 1))
    return plus, minus


def strip_x_neighbours(one):
    return roll_lanes(one, -1), roll_lanes(one, 1)


def weights_of(diff, ocean, x_pairs):
    (diff_n, ocean_n) = (y_neighbours(diff), y_neighbours(ocean))
    out = []
    for t in range(2):
        near = [(diff_n[0][t], ocean_n[0][t]), (diff_n[1][t], ocean_n[1][t])] + list(x_pairs[t])
        faces = [0.5 * (diff[t] + d) * ocean[t] * o for d, o in near]
        out.append((1.0 - (faces[0] + faces[1] + faces[2] + faces[3]), faces))
    return out


def lateral(one, near, weights):
    centre, faces = weights
    total = centre * one
    for face, value in zip(faces, near):
        total = total + face * value
    return total


def couple(diffused, coef, ocean):
    out = []
    for f in range(F):
        total = None
        for g in range(F):
            if diffused[g] is not None:
                term = coef[g][f] * diffused[g]
                total = term if total is None else total + term
        out.append(ocean * total)
    return out


def step_strips(old, weights, vertical, ocean, coef):
    lane = iota((ROWS, LANES), 1)
    diffused = [[None] * F, [None] * F]
    for f in range(F):
        if old[f] is None:
            continue
        plus, minus = y_neighbours(old[f])
        for t in range(2):
            one = old[f][t]
            x_plus, x_minus = strip_x_neighbours(one)
            below = jnp.where(lane < LANES - 16, roll_lanes(one, -16), 0.0)
            flux = vertical[t] * (below - one)
            above = jnp.where(lane < 16, 0.0, roll_lanes(flux, 16))
            diffused[t][f] = lateral(one, (plus[t], minus[t], x_plus, x_minus), weights[t]) + (flux - above)
    coupled = [couple(diffused[t], coef, ocean[t]) for t in range(2)]
    return [(coupled[0][f], coupled[1][f]) for f in range(F)]


def step_tile(read, write, live, edges, weights, vertical, ocean, coef, tiles):
    above = [[None] * F, [None] * F]
    for l in range(LEV):
        diffused = [[None] * F, [None] * F]
        for f in range(F):
            here = read(f, l) if (f, l) in live else None
            below = read(f, l + 1) if (f, l + 1) in live else None
            near = y_neighbours(here) if here is not None else None
            for t in range(tiles):
                flux = None
                if here is not None and below is not None:
                    flux = vertical(l, t) * (below[t] - here[t])
                elif here is not None:
                    flux = -(vertical(l, t) * here[t])
                elif below is not None:
                    flux = vertical(l, t) * below[t]
                total = None
                if here is not None:
                    x_plus, x_minus = x_neighbours(here[t], edges[f][t], l)
                    total = lateral(here[t], (near[0][t], near[1][t], x_plus, x_minus), weights[t])
                if flux is not None:
                    total = flux if total is None else total + flux
                if above[t][f] is not None:
                    total = -above[t][f] if total is None else total - above[t][f]
                above[t][f] = flux
                diffused[t][f] = total
        for t in range(tiles):
            for f, value in enumerate(couple(diffused[t], coef, ocean[t])):
                write(f, l, t, value)


def kernel(
    sizes,
    innov,
    weight,
    level,
    tile,
    cell,
    land,
    hdiff,
    vdiff,
    coupling,
    ice,
    out,
    innov_v,
    weight_v,
    level_v,
    tile_v,
    cell_v,
    land_v,
    ice_v,
    stat,
    stat_y,
    stat_e,
    stat_x,
    send,
    recv,
    forced,
    forced_y,
    forced_e,
    forced_x,
    state,
    local_sem,
    send_sem,
    recv_sem,
):
    n_ty, n_tx, n_grp = sizes
    ty, tx, grp = lax.axis_index("ty"), lax.axis_index("tx"), lax.axis_index("grp")
    blocks = n_tx * n_grp
    block = tx * n_grp + grp
    right, left = (block + 1) % blocks, (block + blocks - 1) % blocks
    down, up = (ty + 1) % n_ty, (ty + n_ty - 1) % n_ty

    def at(row, column):
        return (row, column // n_grp, column % n_grp)

    partner = (ty, tx, 1 - grp)

    def fetch(src, dst, sem):
        copy = pltpu.make_async_copy(src, dst, local_sem.at[sem])
        copy.start()
        return copy

    def put(src, dst, sem, device):
        pltpu.make_async_remote_copy(
            src_ref=src,
            dst_ref=dst,
            send_sem=send_sem.at[sem],
            recv_sem=recv_sem.at[sem],
            device_id=device,
            device_id_type=MESH,
        ).start()

    def wait(ref, sems, sem):
        pltpu.make_async_copy(ref, ref, sems.at[sem]).wait()

    profile_rows = PROFS * VARS
    loads = []
    for w in range(ITERS):
        loads.append(
            [
                fetch(level.at[w], level_v.at[w], L_LEVEL + w),
                fetch(weight.at[w], weight_v.at[w], L_WEIGHT + w),
                fetch(
                    innov.at[pl.ds(w * profile_rows, profile_rows)],
                    innov_v.at[pl.ds(w * profile_rows, profile_rows)],
                    L_INNOV + w,
                ),
            ]
        )
        if w == 0:
            loads[0] += [fetch(tile, tile_v, L_TILE), fetch(cell, cell_v, L_CELL)]
    ice_here = ice.at[:, :, :, pl.ds(pl.multiple_of(grp * LANES, LANES), LANES)]
    ice_there = ice.at[:, :, :, pl.ds(pl.multiple_of((1 - grp) * LANES, LANES), LANES)]
    static_loads = [
        fetch(land, land_v, L_LAND),
        fetch(hdiff, stat.at[LEV], L_HDIFF),
        fetch(vdiff, stat.at[pl.ds(0, LEV)], L_VDIFF),
        fetch(ice_here, ice_v.at[grp], L_ICE),
    ]

    barrier = pltpu.get_barrier_semaphore()
    around = [(r, c) for c in (right, left) for r in (ty, down, up)] + [(down, block), (up, block)]
    for r, c in around:
        pl.semaphore_signal(barrier, inc=1, device_id=at(r, c), device_id_type=MESH)

    def greet(k, carry):
        pl.semaphore_signal(barrier, inc=1, device_id=(ty, (tx + k) % n_tx, grp), device_id_type=MESH)
        return carry

    lax.fori_loop(1, n_tx, greet, 0)

    def route(w):
        for load in loads[w]:
            load.wait()
        innovs = [innov_v[pl.ds(w * profile_rows + v, PROFS, stride=VARS), :] for v in range(VARS)]
        messages = pack_messages(
            weight_v[w], level_v[w], innovs, tile_v[pl.ds(w, 1), :], cell_v[pl.ds(w, 1), :]
        )
        for j in range(3):
            send[w, :, j, :] = messages[:, j * LANES : (j + 1) * LANES]
        if w == 0:
            pl.semaphore_wait(barrier, n_tx - 1 + len(around))
        own = fetch(send.at[w, tx], recv.at[w, tx], L_OWN + w)

        def to_peer(k, carry):
            peer = (tx + k) % n_tx
            put(send.at[w, peer], recv.at[w, tx], R_ROUTE + w, (ty, peer, grp))
            return carry

        lax.fori_loop(1, n_tx, to_peer, 0)
        return own

    def exchange(rows, rows_y, edges, edges_x, sem_y, sem_x):
        put(rows.at[:, pl.ds(0, 4)], rows_y.at[:, pl.ds(0, 4)], sem_y, at(up, block))
        put(rows.at[:, pl.ds(4, 4)], rows_y.at[:, pl.ds(4, 4)], sem_y, at(down, block))
        for side, column in enumerate((right, left)):
            for slot, r in enumerate((ty, up, down)):
                put(edges.at[side], edges_x.at[side * 3 + slot], sem_x, at(r, column))

    if n_tx < SLOTS:
        recv[...] = jnp.zeros(recv.shape, F32)
    owns = [route(0)]
    put(ice_there, ice_v.at[grp], R_ICE, partner)
    for load in static_loads:
        load.wait()
    ocean_tile = land_v[...].astype(F32)
    stat[LEV + 1] = ocean_tile

    def static_items(ref):
        items = [(0, l, ref[l]) for l in range(LEV)]
        return items + [(1 + j, l, ref[LEV + j]) for j in range(2) for l in range(LEV)]

    last, first = pack_edges(static_items(stat))
    stat_e[0] = last
    stat_e[1] = first
    exchange(stat, stat_y, stat_e, stat_x, R_STAT_Y, R_STAT_X)
    owns.append(route(1))

    def force(w):
        owns[w].wait()
        wait(recv.at[w, pl.ds(0, n_tx - 1)], recv_sem, R_ROUTE + w)
        sums = gather_cells(recv[w, :, 0, :], recv[w, :, 1, :], recv[w, :, 2, :])
        if w == 0:
            wait(ice_v.at[0], recv_sem, R_ICE)
        items = []
        for i, (f, l) in enumerate(FORCED):
            value = sums[i * ROWS : (i + 1) * ROWS] if f < VARS else None
            if l == 0:
                melt = jnp.concatenate([ice_v[0, w, f], ice_v[1, w, f]], axis=0)
                value = melt if value is None else value + melt
            value = ocean_tile * value
            forced[w, i] = value
            items.append((f, l, value))
        last, first = pack_edges(items)
        forced_e[w, 0] = last
        forced_e[w, 1] = first
        exchange(
            forced.at[w], forced_y.at[w], forced_e.at[w], forced_x.at[w], R_F_Y + w, R_F_X + w
        )

    force(0)
    force(1)

    wait(stat_y, recv_sem, R_STAT_Y)
    wait(stat_x, recv_sem, R_STAT_X)
    own_edges = ((stat_e[0], stat_e[1]), pack_edges(static_items(stat_y)))
    vertical_s, diff_s, ocean_s = strips((0, 1, 2), [stat_x[i] for i in range(6)], own_edges)
    diff = (stat[LEV], stat_y[LEV])
    ocean = (stat[LEV + 1], stat_y[LEV + 1])
    x_pairs, x_pairs_s = [], []
    for t in range(2):
        d = x_neighbours(diff[t], edge_pair(diff_s[t]), 0)
        o = x_neighbours(ocean[t], edge_pair(ocean_s[t]), 0)
        x_pairs.append(((d[0], o[0]), (d[1], o[1])))
        d, o = strip_x_neighbours(diff_s[t]), strip_x_neighbours(ocean_s[t])
        x_pairs_s.append(((d[0], o[0]), (d[1], o[1])))
    weights = weights_of(diff, ocean, x_pairs)
    weights_s = weights_of(diff_s, ocean_s, x_pairs_s)
    coef = [[coupling[g, f] + (1.0 if f == g else 0.0) for f in range(F)] for g in range(F)]

    def vertical(l, t):
        return stat[l] if t == 0 else stat_y[l]

    def forced_strips(w):
        wait(forced_y.at[w], recv_sem, R_F_Y + w)
        wait(forced_x.at[w], recv_sem, R_F_X + w)
        halo_items = [(f, l, forced_y[w, i]) for i, (f, l) in enumerate(FORCED)]
        own_edges = ((forced_e[w, 0], forced_e[w, 1]), pack_edges(halo_items))
        return strips(range(ICEV), [forced_x[w, i] for i in range(6)], own_edges)

    index = {item: i for i, item in enumerate(FORCED)}
    whole = {(f, l) for f in range(F) for l in range(LEV)}
    packed = forced_strips(0) + [None]

    def read_forced(f, l):
        return forced[0, index[f, l]], forced_y[0, index[f, l]]

    def reader(slot):
        return lambda f, l: (state[slot, 0, f * LEV + l], state[slot, 1, f * LEV + l])

    def writer(slot):
        def write(f, l, t, value):
            state[slot, t, f * LEV + l] = value

        return write

    def write_out(f, l, t, value):
        out[f, l] = value

    n_steps = ITERS * SUB
    for step in range(n_steps):
        end = step == n_steps - 1
        edges = [None if p is None else (edge_pair(p[0]), edge_pair(p[1])) for p in packed]
        step_tile(
            read_forced if step == 0 else reader(step % 2),
            write_out if end else writer((step + 1) % 2),
            set(FORCED) if step == 0 else whole,
            edges,
            weights,
            vertical,
            ocean,
            coef,
            1 if end else 2,
        )
        if not end:
            packed = step_strips(packed, weights_s, vertical_s, ocean_s, coef)
        if step == SUB - 1:
            slot = (step + 1) % 2
            added = forced_strips(1)
            for f in range(ICEV):
                packed[f] = tuple(packed[f][t] + added[f][t] for t in range(2))
            for i, (f, l) in enumerate(FORCED):
                state[slot, 0, f * LEV + l] += forced[1, i]
                state[slot, 1, f * LEV + l] += forced_y[1, i]

    for w in range(ITERS):
        wait(send.at[w, pl.ds(0, n_tx - 1)], send_sem, R_ROUTE + w)
        wait(forced.at[w], send_sem, R_F_Y + w)
        wait(forced_x.at[w], send_sem, R_F_X + w)
    wait(ice_v.at[0], send_sem, R_ICE)
    wait(stat, send_sem, R_STAT_Y)
    wait(stat_x, send_sem, R_STAT_X)


def per_device(sizes, innov, weight, level, tile, cell, land, hdiff, vdiff, coupling, ice):
    scratch = [
        pltpu.VMEM((ITERS * PROFS * VARS, DEPTH), F32),
        pltpu.VMEM((ITERS, PROFS, DEPTH), F32),
        pltpu.VMEM((ITERS, PROFS, DEPTH), jnp.int32),
        pltpu.VMEM((ITERS, PROFS), jnp.int32),
        pltpu.VMEM((ITERS, PROFS), jnp.int32),
        pltpu.VMEM((ROWS, LANES), jnp.int32),
        pltpu.VMEM((2, ITERS, ICEV, 4, LANES), F32),
        pltpu.VMEM((N_STATIC, ROWS, LANES), F32),
        pltpu.VMEM((N_STATIC, ROWS, LANES), F32),
        pltpu.VMEM((2, ROWS, LANES), F32),
        pltpu.VMEM((6, ROWS, LANES), F32),
        pltpu.VMEM((ITERS, SLOTS, 3, LANES), F32),
        pltpu.VMEM((ITERS, SLOTS, 3, LANES), F32),
        pltpu.VMEM((ITERS, N_FORCED, ROWS, LANES), F32),
        pltpu.VMEM((ITERS, N_FORCED, ROWS, LANES), F32),
        pltpu.VMEM((ITERS, 2, ROWS, LANES), F32),
        pltpu.VMEM((ITERS, 6, ROWS, LANES), F32),
        pltpu.VMEM((2, 2, F * LEV, ROWS, LANES), F32),
        pltpu.SemaphoreType.DMA((N_LOCAL,)),
        pltpu.SemaphoreType.DMA((N_REMOTE,)),
        pltpu.SemaphoreType.DMA((N_REMOTE,)),
    ]
    anywhere = pl.BlockSpec(memory_space=pl.ANY)
    return pl.pallas_call(
        functools.partial(kernel, sizes),
        out_shape=jax.ShapeDtypeStruct((F, LEV, ROWS, LANES), F32),
        in_specs=[anywhere] * 8 + [pl.BlockSpec(memory_space=pltpu.SMEM), anywhere],
        out_specs=pl.BlockSpec(memory_space=pltpu.VMEM),
        scratch_shapes=scratch,
        compiler_params=pltpu.CompilerParams(
            collective_id=0, has_side_effects=True, vmem_limit_bytes=16 * 1024 * 1024
        ),
    )(
        innov.reshape(ITERS * PROFS * VARS, DEPTH),
        weight,
        level,
        tile.reshape(ITERS, PROFS),
        cell,
        land,
        hdiff,
        vdiff,
        coupling,
        ice,
    )


def solution(mesh):
    sizes = tuple(mesh.shape[axis] for axis in ("ty", "tx", "grp"))
    in_specs = (
        P(None, ("ty", "tx", "grp"), None, None),
        P(None, ("ty", "tx", "grp"), None),
        P(None, ("ty", "tx", "grp"), None),
        P(None, ("ty", "tx", "grp"), None),
        P(None, ("ty", "tx", "grp")),
        P("ty", ("tx", "grp")),
        P("ty", ("tx", "grp")),
        P(None, "ty", ("tx", "grp")),
        P(),
        P(None, None, ("ty", "grp"), "tx"),
    )
    out_specs = P(None, None, "ty", ("tx", "grp"))
    return jax.shard_map(
        functools.partial(per_device, sizes), mesh=mesh, in_specs=in_specs, out_specs=out_specs, check_vma=False
    )
```

time: 212 us -> 50.1 us (0.24)
  starting transfers between devices: 88.5 us -> 0 us
  waiting for transfers between devices: 85.6 us -> 0 us
  Pallas kernels: 0 us -> 41.7 us
  other arithmetic: 13.8 us -> 0 us
  local copies, waits for them, and re-layouts: 17.9 us -> 7.69 us
  matrix products: 3.43 us -> 0 us
    ppermute x16 -> x0, waiting for transfers between devices: 56.6 us -> none  [the longest x8 34.1 us: extended(): lax.ppermute(lax.slice_in_dim(block, block.shape[dim] - width, None, axis...]
    ppermute x16 -> x0, starting transfers between devices: 49.8 us -> none  [the longest x8 25.5 us: extended(): lax.ppermute(lax.slice_in_dim(block, 0, width, axis=dim), axis, backward)]
    pallas_call x0 -> x1, Pallas kernels: none -> 41.7 us  [per_device(): pl.pallas_call(functools.partial(kernel, sizes), out_shape=jax.ShapeDtype...]
    all_to_all x5 -> x0, starting transfers between devices: 38.7 us -> none  [the longest x2 25.1 us: per_device(): lax.all_to_all(cell_slots, 'tx', split_axis=1, concat_axis=1, tiled=True)]
    all_to_all x5 -> x0, waiting for transfers between devices: 29 us -> none  [the longest x2 14.1 us: per_device(): lax.all_to_all(cell_slots, 'tx', split_axis=1, concat_axis=1, tiled=True)]
    scatter-add x4 -> x0, other arithmetic: 6.69 us -> none  [the longest x2 6.66 us: per_device(): grid = empty_grid.at[:, got_cells[0].astype(jnp.int32)].add(got_payload)]
    scatter x4 -> x0, local copies, waits for them, and re-layouts: 3.84 us -> none  [the longest x2 1.95 us: per_device(): cell_slots = jnp.zeros((1, n_columns * capacity), jnp.float32).at[0, slot...]
    dot_general x6 -> x0, matrix products: 3.43 us -> none  [the longest x4 2.24 us: advance(): jnp.einsum('gf,glyx->flyx', coupling, diffused, precision=EXACT_DOT)]
  transfers between devices with their start and end apart: 21 -> 0, of which waited for: 19 -> 0; matrix products, arithmetic and copies ran while one was open for 10% -> 0% of each run, Pallas kernels for 0% -> 0%
where the time goes in v1:
time: 50.1 us; the launch traced here: 49.4 us
  Pallas kernels  41.7 us (83%)
  local copies, waits for them, and re-layouts  7.69 us (15%)
    pallas_call x1, Pallas kernels, per_device(): pl.pallas_call(functools.partial(kernel, sizes), out_shape=jax.ShapeDtype...  41.7 us
    unnamed x21, local copies, waits for them, and re-layouts  7.69 us

profile of v1, /device:TPU:1, one launch (start us, length us, event | category | flops | bytes accessed | tf_op | source)
XLA Modules:
  0.0 49.4 jit_solution(1777349066695313269)
XLA Ops:
  0.0 0.0 copy-start.9
  0.0 0.0 copy-start.8
  0.0 0.7 %copy-done.9 = s32[2,128]{1,0:T(2,128)S(1)} copy-done((s32[2,128]{1,0:T(2,128)S(1)}, s32[2,128]{1,0:T(2,128)}, u32[]{:S(2)}) %copy-start.9) | copy-done | bytes 1048
  0.7 0.0 copy-done.8
  0.7 0.0 copy-start
  0.7 0.9 %copy-done = f32[2,128,2,128]{3,2,1,0:T(2,128)S(1)} copy-done((f32[2,128,2,128]{3,2,1,0:T(2,128)S(1)}, f32[2,128,2,128]{3,2,1,0:T(2,128)}, u32[]{:S(2)}) %copy-start) | copy-done | bytes 262168
  1.6 0.0 copy-start.1
  1.6 0.9 %copy-done.1 = f32[2,128,128]{2,1,0:T(8,128)S(1)} copy-done((f32[2,128,128]{2,1,0:T(8,128)S(1)}, f32[2,128,128]{2,1,0:T(8,128)}, u32[]{:S(2)}) %copy-start.1) | copy-done | bytes 131096
  2.6 0.0 copy-start.2
  2.6 0.9 %copy-done.2 = s32[2,128,128]{2,1,0:T(8,128)S(1)} copy-done((s32[2,128,128]{2,1,0:T(8,128)S(1)}, s32[2,128,128]{2,1,0:T(8,128)}, u32[]{:S(2)}) %copy-start.2) | copy-done | bytes 131096
  3.5 0.0 copy-start.3
  3.5 0.8 %copy-done.3 = f32[8,8,128]{2,1,0:T(8,128)S(1)} copy-done((f32[8,8,128]{2,1,0:T(8,128)S(1)}, f32[8,8,128]{2,1,0:T(8,128)}, u32[]{:S(2)}) %copy-start.3) | copy-done | bytes 32792
  4.2 0.0 copy-start.4
  4.2 0.8 %copy-done.4 = f32[2,4,4,256]{3,2,1,0:T(4,128)S(1)} copy-done((f32[2,4,4,256]{3,2,1,0:T(4,128)S(1)}, f32[2,4,4,256]{3,2,1,0:T(4,128)}, u32[]{:S(2)}) %copy-start.4) | copy-done | bytes 32792
  5.0 0.0 copy-start.5
  5.0 0.7 %copy-done.5 = s32[8,128]{1,0:T(8,128)S(1)} copy-done((s32[8,128]{1,0:T(8,128)S(1)}, s32[8,128]{1,0:T(8,128)}, u32[]{:S(2)}) %copy-start.5) | copy-done | bytes 4120
  5.7 0.0 copy-start.6
  5.7 0.7 %copy-done.6 = f32[8,128]{1,0:T(8,128)S(1)} copy-done((f32[8,128]{1,0:T(8,128)S(1)}, f32[8,128]{1,0:T(8,128)}, u32[]{:S(2)}) %copy-start.6) | copy-done | bytes 4120
  6.3 0.0 copy-start.7
  6.3 0.7 %copy-done.7 = f32[5,5]{1,0:T(8,128)S(1)} copy-done((f32[5,5]{1,0:T(8,128)S(1)}, f32[5,5]{1,0:T(8,128)}, u32[]{:S(2)}) %copy-start.7) | copy-done | bytes 124
  7.0 41.7 %shard_map.100 = f32[5,8,8,128]{3,2,1,0:T(8,128)S(1)} custom-call(f32[512,128]{1,0:T(8,128)S(1)} %bitcast.2, f32[2,128,128]{2,1,0:T(8,128)S(1)} %copy-done.1, s32[2,128,128]{2,1,0:T(8,128)S(1)} %copy-done.2, s32[2,128]{1,0:T(2,128)S(1)} %bitcast.3, s32[2,128]{1,0:T(2,128)S(1)} %copy-done.9, s32[8,128]{1,0:T(8,128)S(1)} %copy-done.5, f32[8,128]{1,0:T(8,128)S(1)} %copy-done.6, ...), custom_call_target="tpu_custom_call" | custom-call | tf_op jit(solution)/shard_map/pallas_call | solution.py:540
  48.7 0.7 %copy.12 = f32[5,8,8,128]{3,2,1,0:T(8,128)} copy(f32[5,8,8,128]{3,2,1,0:T(8,128)S(1)} %shard_map.100) | data formatting | bytes 327680
Async XLA Ops:
  0.0 0.7 %copy-start.9 = (s32[2,128]{1,0:T(2,128)S(1)}, s32[2,128]{1,0:T(2,128)}, u32[]{:S(2)}) copy-start(s32[2,128]{1,0:T(2,128)} %cell.1) | copy-start | bytes 3076
  0.0 0.7 %copy-start.8 = (s32[2,128,1]{1,2,0:T(1,128)S(1)}, s32[2,128,1]{1,2,0:T(1,128)}, u32[]{:S(2)}) copy-start(s32[2,128,1]{1,2,0:T(1,128)} %param.13) | copy-start | bytes 3076
  0.7 0.9 %copy-start = (f32[2,128,2,128]{3,2,1,0:T(2,128)S(1)}, f32[2,128,2,128]{3,2,1,0:T(2,128)}, u32[]{:S(2)}) copy-start(f32[2,128,2,128]{3,2,1,0:T(2,128)} %param.10) | copy-start | bytes 786436
  1.6 0.9 %copy-start.1 = (f32[2,128,128]{2,1,0:T(8,128)S(1)}, f32[2,128,128]{2,1,0:T(8,128)}, u32[]{:S(2)}) copy-start(f32[2,128,128]{2,1,0:T(8,128)} %weight.1) | copy-start | bytes 393220
  2.6 0.9 %copy-start.2 = (s32[2,128,128]{2,1,0:T(8,128)S(1)}, s32[2,128,128]{2,1,0:T(8,128)}, u32[]{:S(2)}) copy-start(s32[2,128,128]{2,1,0:T(8,128)} %level.1) | copy-start | bytes 393220
  3.5 0.8 %copy-start.3 = (f32[8,8,128]{2,1,0:T(8,128)S(1)}, f32[8,8,128]{2,1,0:T(8,128)}, u32[]{:S(2)}) copy-start(f32[8,8,128]{2,1,0:T(8,128)} %vdiff.1) | copy-start | bytes 98308
  4.2 0.8 %copy-start.4 = (f32[2,4,4,256]{3,2,1,0:T(4,128)S(1)}, f32[2,4,4,256]{3,2,1,0:T(4,128)}, u32[]{:S(2)}) copy-start(f32[2,4,4,256]{3,2,1,0:T(4,128)} %ice.1) | copy-start | bytes 98308
  5.0 0.7 %copy-start.5 = (s32[8,128]{1,0:T(8,128)S(1)}, s32[8,128]{1,0:T(8,128)}, u32[]{:S(2)}) copy-start(s32[8,128]{1,0:T(8,128)} %land.1) | copy-start | bytes 12292
  5.7 0.7 %copy-start.6 = (f32[8,128]{1,0:T(8,128)S(1)}, f32[8,128]{1,0:T(8,128)}, u32[]{:S(2)}) copy-start(f32[8,128]{1,0:T(8,128)} %hdiff.1) | copy-start | bytes 12292
  6.3 0.7 %copy-start.7 = (f32[5,5]{1,0:T(8,128)S(1)}, f32[5,5]{1,0:T(8,128)}, u32[]{:S(2)}) copy-start(f32[5,5]{1,0:T(8,128)} %coupling.1) | copy-start | bytes 304

commit v2 on v1

--- a/solution.py
+++ b/solution.py
@@ -27,11 +27,15 @@
 
 FORCED = [(f, l) for f in range(VARS) for l in range(LEV)] + [(f, 0) for f in range(VARS, ICEV)]
 
-L_LEVEL, L_WEIGHT, L_INNOV = 0, 2, 4
-L_TILE, L_CELL, L_LAND, L_HDIFF, L_VDIFF, L_ICE, L_OWN = 6, 7, 8, 9, 10, 11, 12
-N_LOCAL = 14
-R_ROUTE, R_ICE, R_STAT_Y, R_STAT_X, R_F_Y, R_F_X = 0, 2, 3, 4, 5, 7
-N_REMOTE = 9
+L_LEVEL, L_WEIGHT, L_INNOV, L_TILE, L_CELL, L_LAND, L_HDIFF, L_VDIFF, L_ICE, L_COUPLING, L_OWN = range(11)
+N_LOCAL = 11
+R_ROUTE, R_ICE, R_STAT_Y, R_STAT_X, R_FORCED_Y, R_FORCED_RIGHT, R_FORCED_LEFT = range(7)
+R_BORDER, R_BORDER_ICE, R_BORDER_LAND = range(7, 10)
+N_REMOTE = 10
+
+RANK_ROWS = 4
+RANKS = 4
+MESSAGE = RANK_ROWS + 1
 
 
 def iota(shape, axis):
@@ -53,74 +57,90 @@
     return lax.dot_general(a, b, NT, preferred_element_type=F32)
 
 
-def pack_messages(weight, level, innovs, tile, cell):
+def level_sums(weight, level, innovs):
     level_t = level.T
-    columns = []
+    out = []
     for innov in innovs:
         weighted_t = (weight * innov).T
         rows = [
             jnp.sum(jnp.where(level_t == l, weighted_t, 0.0), axis=0, keepdims=True) for l in range(LEV)
         ]
-        columns.append(jnp.concatenate(rows, axis=0))
-    named = tile == iota((SLOTS, PROFS), 0)
-    named_f = named.astype(F32)
-    named_b = named_f.astype(BF16)
+        out.append(jnp.concatenate(rows, axis=0))
+    return out
+
+
+def rank_in_tile(tile):
+    named = (tile == iota((SLOTS, PROFS), 0)).astype(F32)
     before = (iota((PROFS, PROFS), 0) < iota((PROFS, PROFS), 1)).astype(F32).astype(BF16)
-    counts = lax.dot_general(named_b, before, (((1,), (0,)), ((), ())), preferred_element_type=F32)
-    rank = jnp.sum(named_f * counts, axis=0, keepdims=True).astype(jnp.int32)
-    cell_y = (cell // LANES).astype(F32)
-    cell_x = (cell % LANES).astype(F32)
-    high, low = [], []
-    parts = []
-    for column in columns:
-        top = column.astype(BF16).astype(F32)
-        parts.append((top, column - top))
-    for upper in range(2):
-        for top, rest in parts:
-            for r in range(8):
-                here = rank == upper * 8 + r
-                high.append(jnp.where(here, top, 0.0))
-                low.append(jnp.where(here, rest, 0.0))
+    counts = lax.dot_general(
+        named.astype(BF16), before, (((1,), (0,)), ((), ())), preferred_element_type=F32
+    )
+    return named.astype(BF16), jnp.sum(named * counts, axis=0, keepdims=True).astype(jnp.int32)
+
+
+def pack_messages(columns, tiles, cells):
     row = iota((8, PROFS), 0)
     zero = jnp.zeros((8, PROFS), F32)
-    for r in range(8):
-        first, second = rank == r, rank == r + 8
-        block = jnp.where(jnp.logical_and(row == 0, first), cell_y, 0.0)
-        block = jnp.where(jnp.logical_and(row == 1, first), cell_x, block)
-        block = jnp.where(jnp.logical_and(row == 2, second), cell_y, block)
-        block = jnp.where(jnp.logical_and(row == 3, second), cell_x, block)
-        high.append(block)
-        low.append(zero)
-    high += [zero] * 8
-    low += [zero] * 8
+    named, ranks, tops, rests, yx = [], [], [], [], []
+    for w in range(ITERS):
+        n, rank = rank_in_tile(tiles[w])
+        named += [n, n]
+        ranks.append(rank)
+        top = [c.astype(BF16).astype(F32) for c in columns[w]]
+        tops.append(top)
+        rests.append([c - t for c, t in zip(columns[w], top)])
+        cell = cells[w]
+        yx.append(jnp.where(row % 2 == 0, (cell // LANES).astype(F32), (cell % LANES).astype(F32)))
+    high = [[], []]
+    low = [[], []]
+
+    def add(w, top, rest):
+        for u in range(ITERS):
+            high[u].append(top if u == w else zero)
+            low[u].append(rest if u == w else zero)
+
+    for upper in range(RANK_ROWS):
+        for w in range(ITERS):
+            for v in range(VARS):
+                for r in range(RANKS):
+                    here = ranks[w] == upper * RANKS + r
+                    add(w, jnp.where(here, tops[w][v], 0.0), jnp.where(here, rests[w][v], 0.0))
+    for upper in range(RANK_ROWS):
+        for w in range(ITERS):
+            add(w, jnp.where(ranks[w] == upper * RANKS + row // 2, yx[w], 0.0), zero)
+        add(0, zero, zero)
+        add(0, zero, zero)
     values = jnp.concatenate(
-        [jnp.concatenate(high, axis=0).astype(BF16), jnp.concatenate(low, axis=0).astype(BF16)], axis=1
+        [jnp.concatenate(part[w], axis=0).astype(BF16) for w in range(ITERS) for part in (high, low)], axis=1
     )
-    return dot_nt(jnp.concatenate([named_b, named_b], axis=1), values)
-
-
-def gather_cells(first, second, cells):
-    got = jnp.concatenate([first, second, roll_lanes(first, -8), roll_lanes(second, -8)], axis=0).T
-    where_ = jnp.concatenate(
-        [cells, roll_lanes(cells, -2), roll_lanes(cells, -8), roll_lanes(cells, -10)], axis=0
-    ).T
+    return dot_nt(jnp.concatenate(named, axis=1), values)
+
+
+def gather_cells(received):
+    got = jnp.concatenate([received(j) for j in range(RANK_ROWS)], axis=0).T
+    cells = received(RANK_ROWS)
+    where_ = jnp.concatenate([roll_lanes(cells, -32 * j) for j in range(RANK_ROWS)], axis=0).T
     top = got.astype(BF16).astype(F32)
     rest = got - top
     y_of_row = iota((ROWS, LANES), 0).astype(F32)
     x_of_row = iota((LANES, LANES), 0).astype(F32)
-    left, right = [], []
-    for r in range(0, 8, 2):
-        y_here = where_[r * 8 : r * 8 + 1] == y_of_row
-        x_here = (where_[r * 8 + 1 : r * 8 + 2] == x_of_row).astype(F32).astype(BF16)
-        for part in (top, rest):
-            blocks = []
-            for v in range(VARS):
-                for l in range(LEV):
-                    at = v * 64 + r * 8 + l
-                    blocks.append(jnp.where(y_here, part[at : at + 1], 0.0))
-            left.append(jnp.concatenate(blocks, axis=0).astype(BF16))
-            right.append(x_here)
-    return dot_nt(jnp.concatenate(left, axis=1), jnp.concatenate(right, axis=1))
+    out = []
+    for w in range(ITERS):
+        left, right = [], []
+        for r in range(RANKS):
+            at = (w * RANKS + r) * 2
+            y_here = where_[at : at + 1] == y_of_row
+            x_here = (where_[at + 1 : at + 2] == x_of_row).astype(F32).astype(BF16)
+            for part in (top, rest):
+                blocks = []
+                for v in range(VARS):
+                    for l in range(LEV):
+                        at = w * 64 + v * 32 + r * LEV + l
+                        blocks.append(jnp.where(y_here, part[at : at + 1], 0.0))
+                left.append(jnp.concatenate(blocks, axis=0).astype(BF16))
+                right.append(x_here)
+        out.append(dot_nt(jnp.concatenate(left, axis=1), jnp.concatenate(right, axis=1)))
+    return out
 
 
 def pack_edges(items):
@@ -277,6 +297,7 @@
     tile_v,
     cell_v,
     land_v,
+    coupling_v,
     ice_v,
     stat,
     stat_y,
@@ -288,10 +309,15 @@
     forced_y,
     forced_e,
     forced_x,
+    border,
+    border_ice,
+    border_land,
+    border_e,
     state,
     local_sem,
     send_sem,
     recv_sem,
+    later_sem,
 ):
     n_ty, n_tx, n_grp = sizes
     ty, tx, grp = lax.axis_index("ty"), lax.axis_index("tx"), lax.axis_index("grp")
@@ -303,7 +329,13 @@
     def at(row, column):
         return (row, column // n_grp, column % n_grp)
 
-    partner = (ty, tx, 1 - grp)
+    half = n_tx // 2
+    z = tx % half
+    at_first = jnp.logical_and(z == 0, grp == 0)
+    at_last = jnp.logical_and(z == half - 1, grp == 1)
+
+    def z_of(column):
+        return (column // n_grp) % half
 
     def fetch(src, dst, sem):
         copy = pltpu.make_async_copy(src, dst, local_sem.at[sem])
@@ -323,79 +355,120 @@
     def wait(ref, sems, sem):
         pltpu.make_async_copy(ref, ref, sems.at[sem]).wait()
 
-    profile_rows = PROFS * VARS
-    loads = []
-    for w in range(ITERS):
-        loads.append(
-            [
-                fetch(level.at[w], level_v.at[w], L_LEVEL + w),
-                fetch(weight.at[w], weight_v.at[w], L_WEIGHT + w),
-                fetch(
-                    innov.at[pl.ds(w * profile_rows, profile_rows)],
-                    innov_v.at[pl.ds(w * profile_rows, profile_rows)],
-                    L_INNOV + w,
-                ),
-            ]
-        )
-        if w == 0:
-            loads[0] += [fetch(tile, tile_v, L_TILE), fetch(cell, cell_v, L_CELL)]
+    def signal(sem, device):
+        pl.semaphore_signal(sem, inc=1, device_id=device, device_id_type=MESH)
+
+    def peers(low, high, act):
+        def one(i, carry):
+            for side in range(2):
+                peer = i + side * half
+
+                @pl.when(peer != tx)
+                def _():
+                    act(peer)
+
+            return carry
+
+        lax.fori_loop(low, high, one, 0)
+
+    if n_tx < SLOTS:
+        recv[...] = jnp.zeros(recv.shape, F32)
+        border[...] = jnp.zeros(border.shape, F32)
+
+    loads = [
+        fetch(level, level_v, L_LEVEL),
+        fetch(weight, weight_v, L_WEIGHT),
+        fetch(innov, innov_v, L_INNOV),
+        fetch(tile, tile_v, L_TILE),
+        fetch(cell, cell_v, L_CELL),
+    ]
     ice_here = ice.at[:, :, :, pl.ds(pl.multiple_of(grp * LANES, LANES), LANES)]
     ice_there = ice.at[:, :, :, pl.ds(pl.multiple_of((1 - grp) * LANES, LANES), LANES)]
+    ice_last = ice.at[:, :, :, pl.ds((n_grp - 1) * LANES, LANES)]
     static_loads = [
         fetch(land, land_v, L_LAND),
         fetch(hdiff, stat.at[LEV], L_HDIFF),
         fetch(vdiff, stat.at[pl.ds(0, LEV)], L_VDIFF),
         fetch(ice_here, ice_v.at[grp], L_ICE),
+        fetch(coupling, coupling_v, L_COUPLING),
     ]
 
     barrier = pltpu.get_barrier_semaphore()
-    around = [(r, c) for c in (right, left) for r in (ty, down, up)] + [(down, block), (up, block)]
-    for r, c in around:
-        pl.semaphore_signal(barrier, inc=1, device_id=at(r, c), device_id_type=MESH)
-
-    def greet(k, carry):
-        pl.semaphore_signal(barrier, inc=1, device_id=(ty, (tx + k) % n_tx, grp), device_id_type=MESH)
-        return carry
-
-    lax.fori_loop(1, n_tx, greet, 0)
-
-    def route(w):
-        for load in loads[w]:
-            load.wait()
-        innovs = [innov_v[pl.ds(w * profile_rows + v, PROFS, stride=VARS), :] for v in range(VARS)]
-        messages = pack_messages(
-            weight_v[w], level_v[w], innovs, tile_v[pl.ds(w, 1), :], cell_v[pl.ds(w, 1), :]
+    z_right, z_left = z_of(right), z_of(left)
+    peers(z, half, lambda peer: signal(barrier, (ty, peer, grp)))
+    signal(barrier, at(down, block))
+    signal(barrier, at(up, block))
+    for column, z_there in ((right, z_right), (left, z_left)):
+
+        @pl.when(z_there >= z)
+        def _():
+            for r in (ty, down, up):
+                signal(barrier, at(r, column))
+
+    @pl.when(at_first)
+    def _():
+        def source(k, carry):
+            signal(barrier, (ty, k, 1))
+            return carry
+
+        lax.fori_loop(0, n_tx, source, 0)
+        signal(barrier, (ty, (tx + n_tx - 1) % n_tx, 0))
+
+    earlier = 1 + 2 * z + 2 + jnp.where(z_right <= z, 3, 0) + jnp.where(z_left <= z, 3, 0)
+    earlier = earlier + jnp.where(grp == 1, 2, 0)
+    earlier = earlier + jnp.where(jnp.logical_and(z == half - 1, grp == 0), 1, 0)
+    later = 2 * (half - 1 - z) + jnp.where(z_right > z, 3, 0) + jnp.where(z_left > z, 3, 0)
+    pl.semaphore_wait(barrier, earlier)
+    peers(0, z, lambda peer: signal(later_sem, (ty, peer, grp)))
+    for column, z_there in ((right, z_right), (left, z_left)):
+
+        @pl.when(z_there < z)
+        def _():
+            for r in (ty, down, up):
+                signal(later_sem, at(r, column))
+
+    for load in loads:
+        load.wait()
+    columns = [
+        level_sums(
+            weight_v[w],
+            level_v[w],
+            [innov_v[pl.ds(w * PROFS * VARS + v, PROFS, stride=VARS), :] for v in range(VARS)],
         )
-        for j in range(3):
-            send[w, :, j, :] = messages[:, j * LANES : (j + 1) * LANES]
-        if w == 0:
-            pl.semaphore_wait(barrier, n_tx - 1 + len(around))
-        own = fetch(send.at[w, tx], recv.at[w, tx], L_OWN + w)
-
-        def to_peer(k, carry):
-            peer = (tx + k) % n_tx
-            put(send.at[w, peer], recv.at[w, tx], R_ROUTE + w, (ty, peer, grp))
-            return carry
-
-        lax.fori_loop(1, n_tx, to_peer, 0)
-        return own
-
-    def exchange(rows, rows_y, edges, edges_x, sem_y, sem_x):
-        put(rows.at[:, pl.ds(0, 4)], rows_y.at[:, pl.ds(0, 4)], sem_y, at(up, block))
-        put(rows.at[:, pl.ds(4, 4)], rows_y.at[:, pl.ds(4, 4)], sem_y, at(down, block))
-        for side, column in enumerate((right, left)):
-            for slot, r in enumerate((ty, up, down)):
-                put(edges.at[side], edges_x.at[side * 3 + slot], sem_x, at(r, column))
-
-    if n_tx < SLOTS:
-        recv[...] = jnp.zeros(recv.shape, F32)
-    owns = [route(0)]
-    put(ice_there, ice_v.at[grp], R_ICE, partner)
+        for w in range(ITERS)
+    ]
+    messages = pack_messages(
+        columns, [tile_v[pl.ds(w, 1), :] for w in range(ITERS)], [cell_v[pl.ds(w, 1), :] for w in range(ITERS)]
+    )
+    for j in range(MESSAGE):
+        send[:, j, :] = messages[:, j * LANES : (j + 1) * LANES]
+
+    def route(peer):
+        put(send.at[peer], recv.at[tx], R_ROUTE, (ty, peer, grp))
+
+    @pl.when(grp == 1)
+    def _():
+        for side in range(2):
+            last = half - 1 + side * half
+            put(send.at[last], border.at[tx], R_BORDER, (ty, (last + 1) % n_tx, 0))
+
+    peers(0, z + 1, route)
+    own = fetch(send.at[tx], recv.at[tx], L_OWN)
     for load in static_loads:
         load.wait()
     ocean_tile = land_v[...].astype(F32)
     stat[LEV + 1] = ocean_tile
 
+    @pl.when(z == half - 1)
+    def _():
+        put(ice_last, border_ice.at[grp], R_BORDER_ICE, (ty, (tx + 1) % n_tx, 0))
+
+    @pl.when(at_last)
+    def _():
+        put(stat.at[LEV + 1], border_land, R_BORDER_LAND, (ty, (tx + 1) % n_tx, 0))
+
+    put(ice_there, ice_v.at[grp], R_ICE, (ty, tx, 1 - grp))
+
     def static_items(ref):
         items = [(0, l, ref[l]) for l in range(LEV)]
         return items + [(1 + j, l, ref[LEV + j]) for j in range(2) for l in range(LEV)]
@@ -403,33 +476,74 @@
     last, first = pack_edges(static_items(stat))
     stat_e[0] = last
     stat_e[1] = first
-    exchange(stat, stat_y, stat_e, stat_x, R_STAT_Y, R_STAT_X)
-    owns.append(route(1))
-
-    def force(w):
-        owns[w].wait()
-        wait(recv.at[w, pl.ds(0, n_tx - 1)], recv_sem, R_ROUTE + w)
-        sums = gather_cells(recv[w, :, 0, :], recv[w, :, 1, :], recv[w, :, 2, :])
-        if w == 0:
-            wait(ice_v.at[0], recv_sem, R_ICE)
-        items = []
-        for i, (f, l) in enumerate(FORCED):
-            value = sums[i * ROWS : (i + 1) * ROWS] if f < VARS else None
-            if l == 0:
-                melt = jnp.concatenate([ice_v[0, w, f], ice_v[1, w, f]], axis=0)
-                value = melt if value is None else value + melt
-            value = ocean_tile * value
-            forced[w, i] = value
-            items.append((f, l, value))
-        last, first = pack_edges(items)
-        forced_e[w, 0] = last
-        forced_e[w, 1] = first
-        exchange(
-            forced.at[w], forced_y.at[w], forced_e.at[w], forced_x.at[w], R_F_Y + w, R_F_X + w
-        )
-
-    force(0)
-    force(1)
+
+
+    @pl.when(later > 0)
+    def _():
+        pl.semaphore_wait(later_sem, later)
+
+    peers(z + 1, half, route)
+
+    def exchange_y(rows, rows_y, sem):
+        put(rows.at[:, pl.ds(0, 4)], rows_y.at[:, pl.ds(0, 4)], sem, at(up, block))
+        put(rows.at[:, pl.ds(4, 4)], rows_y.at[:, pl.ds(4, 4)], sem, at(down, block))
+
+    exchange_y(stat, stat_y, R_STAT_Y)
+    for side, column in enumerate((right, left)):
+        for slot, r in enumerate((ty, up, down)):
+            put(stat_e.at[side], stat_x.at[side * 3 + slot], R_STAT_X, at(r, column))
+
+    def force(received, melt_of, ocean_of):
+        sums = gather_cells(received)
+        rows = []
+        for w in range(ITERS):
+            rows.append([])
+            for i, (f, l) in enumerate(FORCED):
+                value = sums[w][i * ROWS : (i + 1) * ROWS] if f < VARS else None
+                if l == 0:
+                    melt = jnp.concatenate([melt_of[0, w, f], melt_of[1, w, f]], axis=0)
+                    value = melt if value is None else value + melt
+                rows[w].append(ocean_of * value)
+        return rows
+
+    def edges_of(rows):
+        return pack_edges([(f, l, rows[i]) for i, (f, l) in enumerate(FORCED)])
+
+    own.wait()
+    wait(recv.at[pl.ds(0, n_tx - 1)], recv_sem, R_ROUTE)
+    wait(ice_v.at[0], recv_sem, R_ICE)
+    rows = force(lambda j: recv[:, j, :], ice_v, ocean_tile)
+    for w in range(ITERS):
+        for i in range(N_FORCED):
+            forced[w * N_FORCED + i] = rows[w][i]
+    exchange_y(forced, forced_y, R_FORCED_Y)
+    for w in range(ITERS):
+        last, first = edges_of(rows[w])
+        forced_e[0, w] = last
+        forced_e[1, w] = first
+
+    def exchange_x(side, column, sem):
+        for slot, r in enumerate((ty, up, down)):
+            put(forced_e.at[side], forced_x.at[side * 3 + slot], sem, at(r, column))
+
+    exchange_x(1, left, R_FORCED_LEFT)
+
+    @pl.when(jnp.logical_not(at_last))
+    def _():
+        exchange_x(0, right, R_FORCED_RIGHT)
+
+    @pl.when(at_first)
+    def _():
+        wait(border.at[pl.ds(0, n_tx)], recv_sem, R_BORDER)
+        wait(border_ice, recv_sem, R_BORDER_ICE)
+        wait(border_land, recv_sem, R_BORDER_LAND)
+        beyond = force(lambda j: border[:, j, :], border_ice, border_land[...])
+        for w in range(ITERS):
+            edge = edges_of(beyond[w])[0]
+            border_e[w] = edge
+            forced_x[0, w] = edge
+        for slot, r in ((1, up), (2, down)):
+            put(border_e, forced_x.at[slot], R_FORCED_RIGHT, at(r, block))
 
     wait(stat_y, recv_sem, R_STAT_Y)
     wait(stat_x, recv_sem, R_STAT_X)
@@ -446,24 +560,39 @@
         x_pairs_s.append(((d[0], o[0]), (d[1], o[1])))
     weights = weights_of(diff, ocean, x_pairs)
     weights_s = weights_of(diff_s, ocean_s, x_pairs_s)
-    coef = [[coupling[g, f] + (1.0 if f == g else 0.0) for f in range(F)] for g in range(F)]
+    coef = [
+        [
+            jnp.broadcast_to(coupling_v[g : g + 1, f : f + 1], (ROWS, LANES)) + (1.0 if f == g else 0.0)
+            for f in range(F)
+        ]
+        for g in range(F)
+    ]
 
     def vertical(l, t):
         return stat[l] if t == 0 else stat_y[l]
 
+    wait(forced_y, recv_sem, R_FORCED_Y)
+    wait(forced_x.at[pl.ds(3, 3)], recv_sem, R_FORCED_LEFT)
+
+    @pl.when(at_first)
+    def _():
+        wait(forced_x.at[pl.ds(1, 2)], recv_sem, R_FORCED_RIGHT)
+
+    @pl.when(jnp.logical_not(at_first))
+    def _():
+        wait(forced_x.at[pl.ds(0, 3)], recv_sem, R_FORCED_RIGHT)
+
     def forced_strips(w):
-        wait(forced_y.at[w], recv_sem, R_F_Y + w)
-        wait(forced_x.at[w], recv_sem, R_F_X + w)
-        halo_items = [(f, l, forced_y[w, i]) for i, (f, l) in enumerate(FORCED)]
-        own_edges = ((forced_e[w, 0], forced_e[w, 1]), pack_edges(halo_items))
-        return strips(range(ICEV), [forced_x[w, i] for i in range(6)], own_edges)
+        halo = edges_of([forced_y[w * N_FORCED + i] for i in range(N_FORCED)])
+        own_edges = ((forced_e[0, w], forced_e[1, w]), halo)
+        return strips(range(ICEV), [forced_x[i, w] for i in range(6)], own_edges)
 
     index = {item: i for i, item in enumerate(FORCED)}
     whole = {(f, l) for f in range(F) for l in range(LEV)}
     packed = forced_strips(0) + [None]
 
     def read_forced(f, l):
-        return forced[0, index[f, l]], forced_y[0, index[f, l]]
+        return forced[index[f, l]], forced_y[index[f, l]]
 
     def reader(slot):
         return lambda f, l: (state[slot, 0, f * LEV + l], state[slot, 1, f * LEV + l])
@@ -500,16 +629,35 @@
             for f in range(ICEV):
                 packed[f] = tuple(packed[f][t] + added[f][t] for t in range(2))
             for i, (f, l) in enumerate(FORCED):
-                state[slot, 0, f * LEV + l] += forced[1, i]
-                state[slot, 1, f * LEV + l] += forced_y[1, i]
-
-    for w in range(ITERS):
-        wait(send.at[w, pl.ds(0, n_tx - 1)], send_sem, R_ROUTE + w)
-        wait(forced.at[w], send_sem, R_F_Y + w)
-        wait(forced_x.at[w], send_sem, R_F_X + w)
+                state[slot, 0, f * LEV + l] += forced[N_FORCED + i]
+                state[slot, 1, f * LEV + l] += forced_y[N_FORCED + i]
+
+    wait(send.at[pl.ds(0, n_tx - 1)], send_sem, R_ROUTE)
     wait(ice_v.at[0], send_sem, R_ICE)
     wait(stat, send_sem, R_STAT_Y)
     wait(stat_x, send_sem, R_STAT_X)
+    wait(forced, send_sem, R_FORCED_Y)
+    wait(forced_x.at[pl.ds(0, 3)], send_sem, R_FORCED_LEFT)
+
+    @pl.when(jnp.logical_not(at_last))
+    def _():
+        wait(forced_x.at[pl.ds(0, 3)], send_sem, R_FORCED_RIGHT)
+
+    @pl.when(at_first)
+    def _():
+        wait(forced_x.at[pl.ds(0, 2)], send_sem, R_FORCED_RIGHT)
+
+    @pl.when(grp == 1)
+    def _():
+        wait(send.at[pl.ds(0, 2)], send_sem, R_BORDER)
+
+    @pl.when(z == half - 1)
+    def _():
+        wait(border_ice.at[0], send_sem, R_BORDER_ICE)
+
+    @pl.when(at_last)
+    def _():
+        wait(border_land, send_sem, R_BORDER_LAND)
 
 
 def per_device(sizes, innov, weight, level, tile, cell, land, hdiff, vdiff, coupling, ice):
@@ -520,33 +668,29 @@
         pltpu.VMEM((ITERS, PROFS), jnp.int32),
         pltpu.VMEM((ITERS, PROFS), jnp.int32),
         pltpu.VMEM((ROWS, LANES), jnp.int32),
+        pltpu.VMEM((F, F), F32),
         pltpu.VMEM((2, ITERS, ICEV, 4, LANES), F32),
         pltpu.VMEM((N_STATIC, ROWS, LANES), F32),
         pltpu.VMEM((N_STATIC, ROWS, LANES), F32),
         pltpu.VMEM((2, ROWS, LANES), F32),
         pltpu.VMEM((6, ROWS, LANES), F32),
-        pltpu.VMEM((ITERS, SLOTS, 3, LANES), F32),
-        pltpu.VMEM((ITERS, SLOTS, 3, LANES), F32),
-        pltpu.VMEM((ITERS, N_FORCED, ROWS, LANES), F32),
-        pltpu.VMEM((ITERS, N_FORCED, ROWS, LANES), F32),
-        pltpu.VMEM((ITERS, 2, ROWS, LANES), F32),
-        pltpu.VMEM((ITERS, 6, ROWS, LANES), F32),
+        pltpu.VMEM((SLOTS, MESSAGE, LANES), F32),
+        pltpu.VMEM((SLOTS, MESSAGE, LANES), F32),
+        pltpu.VMEM((ITERS * N_FORCED, ROWS, LANES), F32),
+        pltpu.VMEM((ITERS * N_FORCED, ROWS, LANES), F32),
+        pltpu.VMEM((2, ITERS, ROWS, LANES), F32),
+        pltpu.VMEM((6, ITERS, ROWS, LANES), F32),
+        pltpu.VMEM((SLOTS, MESSAGE, LANES), F32),
+        pltpu.VMEM((2, ITERS, ICEV, 4, LANES), F32),
+        pltpu.VMEM((ROWS, LANES), F32),
+        pltpu.VMEM((ITERS, ROWS, LANES), F32),
         pltpu.VMEM((2, 2, F * LEV, ROWS, LANES), F32),
         pltpu.SemaphoreType.DMA((N_LOCAL,)),
         pltpu.SemaphoreType.DMA((N_REMOTE,)),
         pltpu.SemaphoreType.DMA((N_REMOTE,)),
+        pltpu.SemaphoreType.REGULAR,
     ]
-    anywhere = pl.BlockSpec(memory_space=pl.ANY)
-    return pl.pallas_call(
-        functools.partial(kernel, sizes),
-        out_shape=jax.ShapeDtypeStruct((F, LEV, ROWS, LANES), F32),
-        in_specs=[anywhere] * 8 + [pl.BlockSpec(memory_space=pltpu.SMEM), anywhere],
-        out_specs=pl.BlockSpec(memory_space=pltpu.VMEM),
-        scratch_shapes=scratch,
-        compiler_params=pltpu.CompilerParams(
-            collective_id=0, has_side_effects=True, vmem_limit_bytes=16 * 1024 * 1024
-        ),
-    )(
+    operands = (
         innov.reshape(ITERS * PROFS * VARS, DEPTH),
         weight,
         level,
@@ -558,6 +702,17 @@
         coupling,
         ice,
     )
+    anywhere = pl.BlockSpec(memory_space=pltpu.HBM)
+    return pl.pallas_call(
+        functools.partial(kernel, sizes),
+        out_shape=jax.ShapeDtypeStruct((F, LEV, ROWS, LANES), F32),
+        in_specs=[anywhere] * len(operands),
+        out_specs=pl.BlockSpec(memory_space=pltpu.VMEM),
+        scratch_shapes=scratch,
+        compiler_params=pltpu.CompilerParams(
+            collective_id=0, has_side_effects=True, vmem_limit_bytes=16 * 1024 * 1024
+        ),
+    )(*(pltpu.with_memory_space_constraint(operand, pltpu.HBM) for operand in operands))
 
 
 def solution(mesh):

time: 50.1 us -> 36.9 us (0.74); the launches traced: 49.4 us -> 36.7 us
  local copies, waits for them, and re-layouts: 7.69 us -> 0.67 us
  Pallas kernels: 41.7 us -> 36.1 us
    unnamed x21 -> x1, local copies, waits for them, and re-layouts: 7.69 us -> 0.67 us
    pallas_call x1, Pallas kernels: 41.7 us -> 36.1 us  [per_device(): pl.pallas_call(functools.partial(kernel, sizes), out_shape=jax.ShapeDtype...]
where the time goes in v2:
time: 36.9 us; the launch traced here: 36.7 us
  Pallas kernels  36.1 us (98%)
  local copies, waits for them, and re-layouts  0.67 us (2%)
    pallas_call x1, Pallas kernels, per_device(): pl.pallas_call(functools.partial(kernel, sizes), out_shape=jax.ShapeDtype...  36.1 us

profile of v2, /device:TPU:1, one launch (start us, length us, event | category | flops | bytes accessed | tf_op | source)
XLA Modules:
  0.0 36.7 jit_solution(17605933869121626721)
XLA Ops:
  0.0 36.1 %shard_map.100 = f32[5,8,8,128]{3,2,1,0:T(8,128)S(1)} custom-call(f32[512,128]{1,0:T(8,128)} %bitcast.2, f32[2,128,128]{2,1,0:T(8,128)} %weight.1, s32[2,128,128]{2,1,0:T(8,128)} %level.1, s32[2,128]{1,0:T(2,128)} %bitcast.3, s32[2,128]{1,0:T(2,128)} %cell.1, s32[8,128]{1,0:T(8,128)} %land.1, f32[8,128]{1,0:T(8,128)} %hdiff.1, f32[8,8,128]{2,1,0:T(8,128)} %vdiff.1, ...), custom_call_target="tpu_custom_call" | custom-call | tf_op jit(solution)/shard_map/pallas_call | solution.py:706
  36.1 0.7 %copy.12 = f32[5,8,8,128]{3,2,1,0:T(8,128)} copy(f32[5,8,8,128]{3,2,1,0:T(8,128)S(1)} %shard_map.100) | data formatting | bytes 327680

commit v3 on v2

--- a/solution.py
+++ b/solution.py
@@ -30,8 +30,10 @@
 L_LEVEL, L_WEIGHT, L_INNOV, L_TILE, L_CELL, L_LAND, L_HDIFF, L_VDIFF, L_ICE, L_COUPLING, L_OWN = range(11)
 N_LOCAL = 11
 R_ROUTE, R_ICE, R_STAT_Y, R_STAT_X, R_FORCED_Y, R_FORCED_RIGHT, R_FORCED_LEFT = range(7)
-R_BORDER, R_BORDER_ICE, R_BORDER_LAND = range(7, 10)
-N_REMOTE = 10
+R_BORDER, R_BORDER_ICE, R_BORDER_LAND, R_STAT_YE, R_FORCED_YE = range(7, 12)
+N_REMOTE = 12
+GROUPS = 3
+S_NEAR, S_DIAGONAL = GROUPS, GROUPS + 1
 
 RANK_ROWS = 4
 RANKS = 4
@@ -140,6 +142,37 @@
                 left.append(jnp.concatenate(blocks, axis=0).astype(BF16))
                 right.append(x_here)
         out.append(dot_nt(jnp.concatenate(left, axis=1), jnp.concatenate(right, axis=1)))
+    return out
+
+
+def gather_edges(received):
+    got = jnp.concatenate([received(j) for j in range(RANK_ROWS)], axis=0).T
+    cells = received(RANK_ROWS)
+    where_ = jnp.concatenate([roll_lanes(cells, -32 * j) for j in range(RANK_ROWS)], axis=0).T
+    top = got.astype(BF16).astype(F32)
+    rest = got - top
+    row = iota((ROWS, LANES), 0)
+    y_of_row = row.astype(F32)
+    x_of_row = (LANES - 4 + row % 4).astype(F32)
+    zero = jnp.zeros((ROWS, LANES), F32)
+    out = []
+    for w in range(ITERS):
+        left, right = [], []
+        for r in range(RANKS):
+            at = (w * RANKS + r) * 2
+            y_here = (where_[at : at + 1] == y_of_row).astype(F32)
+            x_here = where_[at + 1 : at + 2] == x_of_row
+            for part in (top, rest):
+                blocks = []
+                for l in range(LEV):
+                    at = w * 64 + r * LEV + l
+                    both = jnp.where(row < 4, part[at : at + 1], part[at + 32 : at + 33])
+                    blocks += [jnp.where(x_here, both, 0.0), zero]
+                left.append(y_here)
+                right.append(jnp.concatenate(blocks, axis=0).astype(BF16))
+        out.append(
+            dot_nt(jnp.concatenate(left, axis=1).astype(BF16), jnp.concatenate(right, axis=1))
+        )
     return out
 
 
@@ -309,6 +342,8 @@
     forced_y,
     forced_e,
     forced_x,
+    stat_ye,
+    forced_ye,
     border,
     border_ice,
     border_land,
@@ -317,7 +352,7 @@
     local_sem,
     send_sem,
     recv_sem,
-    later_sem,
+    enter_sem,
 ):
     n_ty, n_tx, n_grp = sizes
     ty, tx, grp = lax.axis_index("ty"), lax.axis_index("tx"), lax.axis_index("grp")
@@ -330,7 +365,7 @@
         return (row, column // n_grp, column % n_grp)
 
     half = n_tx // 2
-    z = tx % half
+    z, side = tx % half, tx // half
     at_first = jnp.logical_and(z == 0, grp == 0)
     at_last = jnp.logical_and(z == half - 1, grp == 1)
 
@@ -360,16 +395,27 @@
 
     def peers(low, high, act):
         def one(i, carry):
-            for side in range(2):
-                peer = i + side * half
-
-                @pl.when(peer != tx)
-                def _():
-                    act(peer)
-
+            for half_of in range(2):
+                act(i + half_of * half)
             return carry
 
         lax.fori_loop(low, high, one, 0)
+
+    def turn_y(row):
+        chip, chips = row // 2, n_ty // 2
+        return 2 * jnp.where(chip < chips // 2, chip, chips + chips // 2 - 1 - chip) + 1 - row % 2
+
+    def turn_x(column):
+        return z_of(column) * 2 + column % n_grp
+
+    nearest = [
+        (at(down, block), turn_y(down) > turn_y(ty)),
+        (at(up, block), turn_y(up) > turn_y(ty)),
+        (at(ty, right), turn_x(right) > turn_x(block)),
+        (at(ty, left), turn_x(left) > turn_x(block)),
+    ]
+    bounds = [0, half // 4, half // 2, half]
+    group = jnp.where(z >= bounds[1], 1, 0) + jnp.where(z >= bounds[2], 1, 0)
 
     if n_tx < SLOTS:
         recv[...] = jnp.zeros(recv.shape, F32)
@@ -394,16 +440,14 @@
     ]
 
     barrier = pltpu.get_barrier_semaphore()
-    z_right, z_left = z_of(right), z_of(left)
-    peers(z, half, lambda peer: signal(barrier, (ty, peer, grp)))
-    signal(barrier, at(down, block))
-    signal(barrier, at(up, block))
-    for column, z_there in ((right, z_right), (left, z_left)):
-
-        @pl.when(z_there >= z)
-        def _():
-            for r in (ty, down, up):
-                signal(barrier, at(r, column))
+    peers(z + 1, half, lambda peer: signal(barrier, (ty, peer, grp)))
+
+    @pl.when(side == 0)
+    def _():
+        signal(barrier, (ty, tx + half, grp))
+
+    for device, after in nearest:
+        pl.when(after)(functools.partial(signal, barrier, device))
 
     @pl.when(at_first)
     def _():
@@ -414,18 +458,27 @@
         lax.fori_loop(0, n_tx, source, 0)
         signal(barrier, (ty, (tx + n_tx - 1) % n_tx, 0))
 
-    earlier = 1 + 2 * z + 2 + jnp.where(z_right <= z, 3, 0) + jnp.where(z_left <= z, 3, 0)
-    earlier = earlier + jnp.where(grp == 1, 2, 0)
+    earlier = 2 * z + side + jnp.where(grp == 1, 2, 0)
     earlier = earlier + jnp.where(jnp.logical_and(z == half - 1, grp == 0), 1, 0)
-    later = 2 * (half - 1 - z) + jnp.where(z_right > z, 3, 0) + jnp.where(z_left > z, 3, 0)
-    pl.semaphore_wait(barrier, earlier)
-    peers(0, z, lambda peer: signal(later_sem, (ty, peer, grp)))
-    for column, z_there in ((right, z_right), (left, z_left)):
-
-        @pl.when(z_there < z)
+    later_near = 0
+    for _, after in nearest:
+        earlier = earlier + jnp.where(after, 0, 1)
+        later_near = later_near + jnp.where(after, 1, 0)
+
+    def await_signals(sem, count):
+        @pl.when(count > 0)
         def _():
-            for r in (ty, down, up):
-                signal(later_sem, at(r, column))
+            pl.semaphore_wait(sem, count)
+
+    await_signals(barrier, earlier)
+    peers(0, z, lambda peer: signal(enter_sem.at[group], (ty, peer, grp)))
+
+    @pl.when(side == 1)
+    def _():
+        signal(enter_sem.at[group], (ty, tx - half, grp))
+
+    for device, after in nearest:
+        pl.when(jnp.logical_not(after))(functools.partial(signal, enter_sem.at[S_NEAR], device))
 
     for load in loads:
         load.wait()
@@ -452,7 +505,12 @@
             last = half - 1 + side * half
             put(send.at[last], border.at[tx], R_BORDER, (ty, (last + 1) % n_tx, 0))
 
-    peers(0, z + 1, route)
+    peers(0, z, route)
+
+    @pl.when(side == 1)
+    def _():
+        route(tx - half)
+
     own = fetch(send.at[tx], recv.at[tx], L_OWN)
     for load in static_loads:
         load.wait()
@@ -467,8 +525,6 @@
     def _():
         put(stat.at[LEV + 1], border_land, R_BORDER_LAND, (ty, (tx + 1) % n_tx, 0))
 
-    put(ice_there, ice_v.at[grp], R_ICE, (ty, tx, 1 - grp))
-
     def static_items(ref):
         items = [(0, l, ref[l]) for l in range(LEV)]
         return items + [(1 + j, l, ref[LEV + j]) for j in range(2) for l in range(LEV)]
@@ -477,54 +533,60 @@
     stat_e[0] = last
     stat_e[1] = first
 
-
-    @pl.when(later > 0)
-    def _():
-        pl.semaphore_wait(later_sem, later)
-
-    peers(z + 1, half, route)
+    def route_later(g):
+        low, high = bounds[g], bounds[g + 1]
+        start = jnp.maximum(z + 1, low)
+        twin = jnp.logical_and(side == 0, group == g)
+        await_signals(enter_sem.at[g], 2 * jnp.maximum(high - start, 0) + jnp.where(twin, 1, 0))
+        peers(start, high, route)
+
+        @pl.when(twin)
+        def _():
+            route(tx + half)
+
+    for g in range(GROUPS - 1):
+        route_later(g)
+    await_signals(enter_sem.at[S_NEAR], later_near)
+    for r in (up, down):
+        signal(enter_sem.at[S_DIAGONAL], at(r, block))
+    put(ice_there, ice_v.at[grp], R_ICE, (ty, tx, 1 - grp))
+    route_later(GROUPS - 1)
+    pl.semaphore_wait(enter_sem.at[S_DIAGONAL], 2)
 
     def exchange_y(rows, rows_y, sem):
-        put(rows.at[:, pl.ds(0, 4)], rows_y.at[:, pl.ds(0, 4)], sem, at(up, block))
-        put(rows.at[:, pl.ds(4, 4)], rows_y.at[:, pl.ds(4, 4)], sem, at(down, block))
+        for r, part in ((up, pl.ds(0, 4)), (down, pl.ds(4, 4))):
+            whole_ = (slice(None),) * (len(rows.shape) - 2)
+            put(rows.at[*whole_, part], rows_y.at[*whole_, part], sem, at(r, block))
 
     exchange_y(stat, stat_y, R_STAT_Y)
-    for side, column in enumerate((right, left)):
+    exchange_y(stat_e, stat_ye, R_STAT_YE)
+    for edge, column in enumerate((right, left)):
         for slot, r in enumerate((ty, up, down)):
-            put(stat_e.at[side], stat_x.at[side * 3 + slot], R_STAT_X, at(r, column))
-
-    def force(received, melt_of, ocean_of):
-        sums = gather_cells(received)
-        rows = []
-        for w in range(ITERS):
-            rows.append([])
-            for i, (f, l) in enumerate(FORCED):
-                value = sums[w][i * ROWS : (i + 1) * ROWS] if f < VARS else None
-                if l == 0:
-                    melt = jnp.concatenate([melt_of[0, w, f], melt_of[1, w, f]], axis=0)
-                    value = melt if value is None else value + melt
-                rows[w].append(ocean_of * value)
-        return rows
-
-    def edges_of(rows):
-        return pack_edges([(f, l, rows[i]) for i, (f, l) in enumerate(FORCED)])
+            put(stat_e.at[edge], stat_x.at[edge * 3 + slot], R_STAT_X, at(r, column))
 
     own.wait()
     wait(recv.at[pl.ds(0, n_tx - 1)], recv_sem, R_ROUTE)
     wait(ice_v.at[0], recv_sem, R_ICE)
-    rows = force(lambda j: recv[:, j, :], ice_v, ocean_tile)
+    sums = gather_cells(lambda j: recv[:, j, :])
+    rows = []
     for w in range(ITERS):
-        for i in range(N_FORCED):
+        rows.append([])
+        for i, (f, l) in enumerate(FORCED):
+            value = sums[w][i * ROWS : (i + 1) * ROWS] if f < VARS else None
+            if l == 0:
+                melt = jnp.concatenate([ice_v[0, w, f], ice_v[1, w, f]], axis=0)
+                value = melt if value is None else value + melt
+            rows[w].append(ocean_tile * value)
             forced[w * N_FORCED + i] = rows[w][i]
     exchange_y(forced, forced_y, R_FORCED_Y)
     for w in range(ITERS):
-        last, first = edges_of(rows[w])
+        last, first = pack_edges([(f, l, rows[w][i]) for i, (f, l) in enumerate(FORCED)])
         forced_e[0, w] = last
         forced_e[1, w] = first
 
-    def exchange_x(side, column, sem):
+    def exchange_x(edge, column, sem):
         for slot, r in enumerate((ty, up, down)):
-            put(forced_e.at[side], forced_x.at[side * 3 + slot], sem, at(r, column))
+            put(forced_e.at[edge], forced_x.at[edge * 3 + slot], sem, at(r, column))
 
     exchange_x(1, left, R_FORCED_LEFT)
 
@@ -532,22 +594,37 @@
     def _():
         exchange_x(0, right, R_FORCED_RIGHT)
 
+    exchange_y(forced_e, forced_ye, R_FORCED_YE)
+
     @pl.when(at_first)
     def _():
+        wait(border_land, recv_sem, R_BORDER_LAND)
+        wait(border_ice, recv_sem, R_BORDER_ICE)
+        lane = iota((ROWS, LANES), 1)
+        ocean_edge = jnp.where(lane < 4, roll_lanes(border_land[...], 4), 0.0)
+        for width in (4, 8, 16, 32, 64):
+            ocean_edge = ocean_edge + roll_lanes(ocean_edge, width)
+        melts = []
+        for w in range(ITERS):
+            melt = jnp.zeros((ROWS, LANES), F32)
+            for f in range(ICEV):
+                tile_of = jnp.concatenate([border_ice[0, w, f], border_ice[1, w, f]], axis=0)
+                here = jnp.logical_and(lane >= 4 * f, lane < 4 * f + 4)
+                melt = jnp.where(here, roll_lanes(tile_of, 4 * f + 4), melt)
+            melts.append(melt)
         wait(border.at[pl.ds(0, n_tx)], recv_sem, R_BORDER)
-        wait(border_ice, recv_sem, R_BORDER_ICE)
-        wait(border_land, recv_sem, R_BORDER_LAND)
-        beyond = force(lambda j: border[:, j, :], border_ice, border_land[...])
+        sums = gather_edges(lambda j: border[:, j, :])
         for w in range(ITERS):
-            edge = edges_of(beyond[w])[0]
+            edge = ocean_edge * (sums[w] + melts[w])
             border_e[w] = edge
             forced_x[0, w] = edge
         for slot, r in ((1, up), (2, down)):
             put(border_e, forced_x.at[slot], R_FORCED_RIGHT, at(r, block))
 
     wait(stat_y, recv_sem, R_STAT_Y)
+    wait(stat_ye, recv_sem, R_STAT_YE)
     wait(stat_x, recv_sem, R_STAT_X)
-    own_edges = ((stat_e[0], stat_e[1]), pack_edges(static_items(stat_y)))
+    own_edges = ((stat_e[0], stat_e[1]), (stat_ye[0], stat_ye[1]))
     vertical_s, diff_s, ocean_s = strips((0, 1, 2), [stat_x[i] for i in range(6)], own_edges)
     diff = (stat[LEV], stat_y[LEV])
     ocean = (stat[LEV + 1], stat_y[LEV + 1])
@@ -572,6 +649,7 @@
         return stat[l] if t == 0 else stat_y[l]
 
     wait(forced_y, recv_sem, R_FORCED_Y)
+    wait(forced_ye, recv_sem, R_FORCED_YE)
     wait(forced_x.at[pl.ds(3, 3)], recv_sem, R_FORCED_LEFT)
 
     @pl.when(at_first)
@@ -583,8 +661,7 @@
         wait(forced_x.at[pl.ds(0, 3)], recv_sem, R_FORCED_RIGHT)
 
     def forced_strips(w):
-        halo = edges_of([forced_y[w * N_FORCED + i] for i in range(N_FORCED)])
-        own_edges = ((forced_e[0, w], forced_e[1, w]), halo)
+        own_edges = ((forced_e[0, w], forced_e[1, w]), (forced_ye[0, w], forced_ye[1, w]))
         return strips(range(ICEV), [forced_x[i, w] for i in range(6)], own_edges)
 
     index = {item: i for i, item in enumerate(FORCED)}
@@ -635,6 +712,8 @@
     wait(send.at[pl.ds(0, n_tx - 1)], send_sem, R_ROUTE)
     wait(ice_v.at[0], send_sem, R_ICE)
     wait(stat, send_sem, R_STAT_Y)
+    wait(stat_ye, send_sem, R_STAT_YE)
+    wait(forced_ye, send_sem, R_FORCED_YE)
     wait(stat_x, send_sem, R_STAT_X)
     wait(forced, send_sem, R_FORCED_Y)
     wait(forced_x.at[pl.ds(0, 3)], send_sem, R_FORCED_LEFT)
@@ -680,6 +759,8 @@
         pltpu.VMEM((ITERS * N_FORCED, ROWS, LANES), F32),
         pltpu.VMEM((2, ITERS, ROWS, LANES), F32),
         pltpu.VMEM((6, ITERS, ROWS, LANES), F32),
+        pltpu.VMEM((2, ROWS, LANES), F32),
+        pltpu.VMEM((2, ITERS, ROWS, LANES), F32),
         pltpu.VMEM((SLOTS, MESSAGE, LANES), F32),
         pltpu.VMEM((2, ITERS, ICEV, 4, LANES), F32),
         pltpu.VMEM((ROWS, LANES), F32),
@@ -688,7 +769,7 @@
         pltpu.SemaphoreType.DMA((N_LOCAL,)),
         pltpu.SemaphoreType.DMA((N_REMOTE,)),
         pltpu.SemaphoreType.DMA((N_REMOTE,)),
-        pltpu.SemaphoreType.REGULAR,
+        pltpu.SemaphoreType.REGULAR((GROUPS + 2,)),
     ]
     operands = (
         innov.reshape(ITERS * PROFS * VARS, DEPTH),

time: 36.9 us -> 36.7 us (level)
  no operation moved by 1% of the time
where the time goes in v3:
time: 36.7 us; the launch traced here: 36.6 us
  Pallas kernels  35.9 us (98%)
  local copies, waits for them, and re-layouts  0.67 us (2%)
    pallas_call x1, Pallas kernels, per_device(): pl.pallas_call(functools.partial(kernel, sizes), out_shape=jax.ShapeDtype...  35.9 us

profile of v3, /device:TPU:1, one launch (start us, length us, event | category | flops | bytes accessed | tf_op | source)
XLA Modules:
  0.0 36.6 jit_solution(945932892609044722)
XLA Ops:
  0.0 35.9 %shard_map.100 = f32[5,8,8,128]{3,2,1,0:T(8,128)S(1)} custom-call(f32[512,128]{1,0:T(8,128)} %bitcast.2, f32[2,128,128]{2,1,0:T(8,128)} %weight.1, s32[2,128,128]{2,1,0:T(8,128)} %level.1, s32[2,128]{1,0:T(2,128)} %bitcast.3, s32[2,128]{1,0:T(2,128)} %cell.1, s32[8,128]{1,0:T(8,128)} %land.1, f32[8,128]{1,0:T(8,128)} %hdiff.1, f32[8,8,128]{2,1,0:T(8,128)} %vdiff.1, ...), custom_call_target="tpu_custom_call" | custom-call | tf_op jit(solution)/shard_map/pallas_call | solution.py:787
  35.9 0.7 %copy.12 = f32[5,8,8,128]{3,2,1,0:T(8,128)} copy(f32[5,8,8,128]{3,2,1,0:T(8,128)S(1)} %shard_map.100) | data formatting | bytes 327680

commit v4 on v3

--- a/solution.py
+++ b/solution.py
@@ -27,13 +27,13 @@
 
 FORCED = [(f, l) for f in range(VARS) for l in range(LEV)] + [(f, 0) for f in range(VARS, ICEV)]
 
-L_LEVEL, L_WEIGHT, L_INNOV, L_TILE, L_CELL, L_LAND, L_HDIFF, L_VDIFF, L_ICE, L_COUPLING, L_OWN = range(11)
-N_LOCAL = 11
+L_LEVEL, L_WEIGHT, L_INNOV, L_TILE, L_CELL, L_LAND, L_HDIFF, L_VDIFF, L_ICE, L_COUPLING, L_OWN, L_BORDER = range(12)
+N_LOCAL = 12
 R_ROUTE, R_ICE, R_STAT_Y, R_STAT_X, R_FORCED_Y, R_FORCED_RIGHT, R_FORCED_LEFT = range(7)
 R_BORDER, R_BORDER_ICE, R_BORDER_LAND, R_STAT_YE, R_FORCED_YE = range(7, 12)
 N_REMOTE = 12
 GROUPS = 3
-S_NEAR, S_DIAGONAL = GROUPS, GROUPS + 1
+S_NEAR, S_BESIDE, S_DIAGONAL = GROUPS, GROUPS + 1, GROUPS + 2
 
 RANK_ROWS = 4
 RANKS = 4
@@ -145,7 +145,7 @@
     return out
 
 
-def gather_edges(received):
+def gather_edges(received, firsts):
     got = jnp.concatenate([received(j) for j in range(RANK_ROWS)], axis=0).T
     cells = received(RANK_ROWS)
     where_ = jnp.concatenate([roll_lanes(cells, -32 * j) for j in range(RANK_ROWS)], axis=0).T
@@ -153,7 +153,6 @@
     rest = got - top
     row = iota((ROWS, LANES), 0)
     y_of_row = row.astype(F32)
-    x_of_row = (LANES - 4 + row % 4).astype(F32)
     zero = jnp.zeros((ROWS, LANES), F32)
     out = []
     for w in range(ITERS):
@@ -161,18 +160,35 @@
         for r in range(RANKS):
             at = (w * RANKS + r) * 2
             y_here = (where_[at : at + 1] == y_of_row).astype(F32)
-            x_here = where_[at + 1 : at + 2] == x_of_row
+            x_here = [where_[at + 1 : at + 2] == (first + row % 4).astype(F32) for first in firsts]
             for part in (top, rest):
-                blocks = []
+                blocks = [[] for _ in firsts]
                 for l in range(LEV):
                     at = w * 64 + r * LEV + l
                     both = jnp.where(row < 4, part[at : at + 1], part[at + 32 : at + 33])
-                    blocks += [jnp.where(x_here, both, 0.0), zero]
+                    for block, here in zip(blocks, x_here):
+                        block += [jnp.where(here, both, 0.0), zero]
                 left.append(y_here)
-                right.append(jnp.concatenate(blocks, axis=0).astype(BF16))
-        out.append(
-            dot_nt(jnp.concatenate(left, axis=1).astype(BF16), jnp.concatenate(right, axis=1))
-        )
+                right.append(jnp.concatenate(sum(blocks, []), axis=0).astype(BF16))
+        sums = dot_nt(jnp.concatenate(left, axis=1).astype(BF16), jnp.concatenate(right, axis=1))
+        out.append([sums[:, i * LANES : (i + 1) * LANES] for i in range(len(firsts))])
+    return out
+
+
+def edge_ocean(ocean, first):
+    lane = iota((ROWS, LANES), 1)
+    out = jnp.where(lane < 4, roll_lanes(ocean, -first), 0.0)
+    for width in (4, 8, 16, 32, 64):
+        out = out + roll_lanes(out, width)
+    return out
+
+
+def edge_melt(melts, first):
+    lane = iota((ROWS, LANES), 1)
+    out = jnp.zeros((ROWS, LANES), F32)
+    for f, melt in enumerate(melts):
+        here = jnp.logical_and(lane >= 4 * f, lane < 4 * f + 4)
+        out = jnp.where(here, roll_lanes(melt, 4 * f - first), out)
     return out
 
 
@@ -345,6 +361,7 @@
     stat_ye,
     forced_ye,
     border,
+    border_edge,
     border_ice,
     border_land,
     border_e,
@@ -366,11 +383,8 @@
 
     half = n_tx // 2
     z, side = tx % half, tx // half
-    at_first = jnp.logical_and(z == 0, grp == 0)
+    at_first = jnp.logical_and(z == 0, grp == 1)
     at_last = jnp.logical_and(z == half - 1, grp == 1)
-
-    def z_of(column):
-        return (column // n_grp) % half
 
     def fetch(src, dst, sem):
         copy = pltpu.make_async_copy(src, dst, local_sem.at[sem])
@@ -405,14 +419,11 @@
         chip, chips = row // 2, n_ty // 2
         return 2 * jnp.where(chip < chips // 2, chip, chips + chips // 2 - 1 - chip) + 1 - row % 2
 
-    def turn_x(column):
-        return z_of(column) * 2 + column % n_grp
-
+    partner = (ty, tx, 1 - grp)
     nearest = [
         (at(down, block), turn_y(down) > turn_y(ty)),
         (at(up, block), turn_y(up) > turn_y(ty)),
-        (at(ty, right), turn_x(right) > turn_x(block)),
-        (at(ty, left), turn_x(left) > turn_x(block)),
+        (partner, grp == 0),
     ]
     bounds = [0, half // 4, half // 2, half]
     group = jnp.where(z >= bounds[1], 1, 0) + jnp.where(z >= bounds[2], 1, 0)
@@ -420,6 +431,37 @@
     if n_tx < SLOTS:
         recv[...] = jnp.zeros(recv.shape, F32)
         border[...] = jnp.zeros(border.shape, F32)
+
+    barrier = pltpu.get_barrier_semaphore()
+    for device, after in nearest:
+        pl.when(after)(functools.partial(signal, barrier, device))
+
+    @pl.when(side == 0)
+    def _():
+        signal(barrier, (ty, tx + half, grp))
+
+    peers(z + 1, half, lambda peer: signal(barrier, (ty, peer, grp)))
+
+    at_border = jnp.logical_and(z == 0, grp == 0)
+
+    @pl.when(at_border)
+    def _():
+        signal(barrier, (ty, (tx + n_tx - 1) % n_tx, 1))
+
+    @pl.when(at_first)
+    def _():
+        signal(barrier, (ty, (tx + n_tx - 1) % n_tx, 0))
+
+    earlier = 2 * z + side + jnp.where(z == half - 1, 1, 0)
+    later_near = 0
+    for _, after in nearest:
+        earlier = earlier + jnp.where(after, 0, 1)
+        later_near = later_near + jnp.where(after, 1, 0)
+
+    def await_signals(sem, count):
+        @pl.when(count > 0)
+        def _():
+            pl.semaphore_wait(sem, count)
 
     loads = [
         fetch(level, level_v, L_LEVEL),
@@ -439,47 +481,6 @@
         fetch(coupling, coupling_v, L_COUPLING),
     ]
 
-    barrier = pltpu.get_barrier_semaphore()
-    peers(z + 1, half, lambda peer: signal(barrier, (ty, peer, grp)))
-
-    @pl.when(side == 0)
-    def _():
-        signal(barrier, (ty, tx + half, grp))
-
-    for device, after in nearest:
-        pl.when(after)(functools.partial(signal, barrier, device))
-
-    @pl.when(at_first)
-    def _():
-        def source(k, carry):
-            signal(barrier, (ty, k, 1))
-            return carry
-
-        lax.fori_loop(0, n_tx, source, 0)
-        signal(barrier, (ty, (tx + n_tx - 1) % n_tx, 0))
-
-    earlier = 2 * z + side + jnp.where(grp == 1, 2, 0)
-    earlier = earlier + jnp.where(jnp.logical_and(z == half - 1, grp == 0), 1, 0)
-    later_near = 0
-    for _, after in nearest:
-        earlier = earlier + jnp.where(after, 0, 1)
-        later_near = later_near + jnp.where(after, 1, 0)
-
-    def await_signals(sem, count):
-        @pl.when(count > 0)
-        def _():
-            pl.semaphore_wait(sem, count)
-
-    await_signals(barrier, earlier)
-    peers(0, z, lambda peer: signal(enter_sem.at[group], (ty, peer, grp)))
-
-    @pl.when(side == 1)
-    def _():
-        signal(enter_sem.at[group], (ty, tx - half, grp))
-
-    for device, after in nearest:
-        pl.when(jnp.logical_not(after))(functools.partial(signal, enter_sem.at[S_NEAR], device))
-
     for load in loads:
         load.wait()
     columns = [
@@ -496,22 +497,7 @@
     for j in range(MESSAGE):
         send[:, j, :] = messages[:, j * LANES : (j + 1) * LANES]
 
-    def route(peer):
-        put(send.at[peer], recv.at[tx], R_ROUTE, (ty, peer, grp))
-
-    @pl.when(grp == 1)
-    def _():
-        for side in range(2):
-            last = half - 1 + side * half
-            put(send.at[last], border.at[tx], R_BORDER, (ty, (last + 1) % n_tx, 0))
-
-    peers(0, z, route)
-
-    @pl.when(side == 1)
-    def _():
-        route(tx - half)
-
-    own = fetch(send.at[tx], recv.at[tx], L_OWN)
+    await_signals(barrier, earlier)
     for load in static_loads:
         load.wait()
     ocean_tile = land_v[...].astype(F32)
@@ -519,11 +505,53 @@
 
     @pl.when(z == half - 1)
     def _():
-        put(ice_last, border_ice.at[grp], R_BORDER_ICE, (ty, (tx + 1) % n_tx, 0))
+        put(ice_last, border_ice.at[grp], R_BORDER_ICE, (ty, (tx + 1) % n_tx, 1))
 
     @pl.when(at_last)
     def _():
-        put(stat.at[LEV + 1], border_land, R_BORDER_LAND, (ty, (tx + 1) % n_tx, 0))
+        put(stat.at[LEV + 1], border_land, R_BORDER_LAND, (ty, (tx + 1) % n_tx, 1))
+
+    for device, after in nearest:
+        pl.when(jnp.logical_not(after))(functools.partial(signal, enter_sem.at[S_NEAR], device))
+
+    @pl.when(jnp.logical_and(grp == 1, z > 0))
+    def _():
+        signal(enter_sem.at[S_BESIDE], (ty, tx - 1, 1))
+
+    def route(peer):
+        put(send.at[peer], recv.at[tx], R_ROUTE, (ty, peer, grp))
+
+    def route_border(first_tx):
+        put(send.at[(first_tx + n_tx - 1) % n_tx], border.at[tx], R_BORDER, (ty, first_tx, 1))
+
+    @pl.when(jnp.logical_and(grp == 1, z > 0))
+    def _():
+        route_border(0)
+        route_border(half)
+
+    @pl.when(jnp.logical_and(at_first, side == 1))
+    def _():
+        route_border(0)
+
+    peers(0, z, route)
+
+    @pl.when(side == 1)
+    def _():
+        route(tx - half)
+
+    peers(0, z, lambda peer: signal(enter_sem.at[group], (ty, peer, grp)))
+
+    @pl.when(side == 1)
+    def _():
+        signal(enter_sem.at[group], (ty, tx - half, grp))
+
+    own = fetch(send.at[tx], recv.at[tx], L_OWN)
+
+    @pl.when(at_first)
+    def _():
+        pltpu.make_async_copy(
+            send.at[(tx + n_tx - 1) % n_tx], border.at[tx], local_sem.at[L_BORDER]
+        ).start()
 
     def static_items(ref):
         items = [(0, l, ref[l]) for l in range(LEV)]
@@ -543,83 +571,104 @@
         @pl.when(twin)
         def _():
             route(tx + half)
+            pl.when(at_first)(functools.partial(route_border, half))
 
     for g in range(GROUPS - 1):
         route_later(g)
     await_signals(enter_sem.at[S_NEAR], later_near)
     for r in (up, down):
         signal(enter_sem.at[S_DIAGONAL], at(r, block))
-    put(ice_there, ice_v.at[grp], R_ICE, (ty, tx, 1 - grp))
+    put(ice_there, ice_v.at[grp], R_ICE, partner)
+
+    def tell():
+        signal(enter_sem.at[S_BESIDE], (ty, (tx + 1) % n_tx, 0))
+
+    soon = jnp.logical_or(z + 1 < bounds[GROUPS - 1], z == half - 1)
+    pl.when(jnp.logical_and(grp == 0, soon))(tell)
     route_later(GROUPS - 1)
-    pl.semaphore_wait(enter_sem.at[S_DIAGONAL], 2)
-
+    pl.when(jnp.logical_and(grp == 0, jnp.logical_not(soon)))(tell)
     def exchange_y(rows, rows_y, sem):
         for r, part in ((up, pl.ds(0, 4)), (down, pl.ds(4, 4))):
             whole_ = (slice(None),) * (len(rows.shape) - 2)
             put(rows.at[*whole_, part], rows_y.at[*whole_, part], sem, at(r, block))
 
+    def exchange_x(edge, column, rows, rows_x, sem):
+        for slot, r in reversed(list(enumerate((ty, up, down)))):
+            put(rows.at[edge], rows_x.at[edge * 3 + slot], sem, at(r, column))
+
+    beside = jnp.where(grp == 0, left, right)
+
+    def meet_beside():
+        await_signals(enter_sem.at[S_BESIDE], jnp.where(jnp.logical_or(grp == 0, z < half - 1), 1, 0))
+        for r in (up, down):
+            signal(enter_sem.at[S_DIAGONAL + 1], at(r, block))
+        pl.semaphore_wait(enter_sem.at[S_DIAGONAL + 1], 2)
+        exchange_x(1 - grp, beside, stat_e, stat_x, R_STAT_X)
+
+    def force_beside():
+        @pl.when(jnp.logical_not(at_last))
+        def _():
+            exchange_x(1 - grp, beside, forced_e, forced_x, R_FORCED_RIGHT + 1 - grp)
+
+    pl.semaphore_wait(enter_sem.at[S_DIAGONAL], 2)
     exchange_y(stat, stat_y, R_STAT_Y)
     exchange_y(stat_e, stat_ye, R_STAT_YE)
-    for edge, column in enumerate((right, left)):
-        for slot, r in enumerate((ty, up, down)):
-            put(stat_e.at[edge], stat_x.at[edge * 3 + slot], R_STAT_X, at(r, column))
+    exchange_x(grp, tx * n_grp + 1 - grp, stat_e, stat_x, R_STAT_X)
+    pl.when(jnp.logical_not(at_border))(meet_beside)
+
+    def melts_of(ref, w):
+        return [jnp.concatenate([ref[0, w, f], ref[1, w, f]], axis=0) for f in range(ICEV)]
+
+    last_cols, first_cols = LANES - 4, 0
+    wait(ice_v.at[0], recv_sem, R_ICE)
+    melts = [melts_of(ice_v, w) for w in range(ITERS)]
+    oceans_e = [edge_ocean(ocean_tile, first) for first in (last_cols, first_cols)]
+    melts_e = [[edge_melt(melts[w], first) for first in (last_cols, first_cols)] for w in range(ITERS)]
+
+    @pl.when(at_first)
+    def _():
+        wait(border_land, recv_sem, R_BORDER_LAND)
+        wait(border_ice, recv_sem, R_BORDER_ICE)
+        border_edge[0] = edge_ocean(border_land[...], last_cols)
+        for w in range(ITERS):
+            border_edge[1 + w] = edge_melt(melts_of(border_ice, w), last_cols)
 
     own.wait()
     wait(recv.at[pl.ds(0, n_tx - 1)], recv_sem, R_ROUTE)
-    wait(ice_v.at[0], recv_sem, R_ICE)
+    sums_e = gather_edges(lambda j: recv[:, j, :], (last_cols, first_cols))
+    for w in range(ITERS):
+        last, first = [oceans_e[i] * (sums_e[w][i] + melts_e[w][i]) for i in range(2)]
+        forced_e[0, w] = last
+        forced_e[1, w] = roll_lanes(first, 4)
+
+    pl.when(jnp.logical_not(at_border))(force_beside)
+    exchange_x(grp, tx * n_grp + 1 - grp, forced_e, forced_x, R_FORCED_RIGHT + grp)
+    exchange_y(forced_e, forced_ye, R_FORCED_YE)
+
+    @pl.when(at_first)
+    def _():
+        wait(border.at[tx], local_sem, L_BORDER)
+        wait(border.at[pl.ds(0, n_tx - 1)], recv_sem, R_BORDER)
+        sums_b = gather_edges(lambda j: border[:, j, :], (last_cols,))
+        for w in range(ITERS):
+            border_e[w] = border_edge[0] * (sums_b[w][0] + border_edge[1 + w])
+        for slot, r in ((1, up), (2, down), (0, ty)):
+            put(border_e, forced_x.at[slot], R_FORCED_RIGHT, (r, tx, 0))
+
     sums = gather_cells(lambda j: recv[:, j, :])
-    rows = []
     for w in range(ITERS):
-        rows.append([])
         for i, (f, l) in enumerate(FORCED):
             value = sums[w][i * ROWS : (i + 1) * ROWS] if f < VARS else None
             if l == 0:
-                melt = jnp.concatenate([ice_v[0, w, f], ice_v[1, w, f]], axis=0)
-                value = melt if value is None else value + melt
-            rows[w].append(ocean_tile * value)
-            forced[w * N_FORCED + i] = rows[w][i]
+                value = melts[w][f] if value is None else value + melts[w][f]
+            forced[w * N_FORCED + i] = ocean_tile * value
     exchange_y(forced, forced_y, R_FORCED_Y)
-    for w in range(ITERS):
-        last, first = pack_edges([(f, l, rows[w][i]) for i, (f, l) in enumerate(FORCED)])
-        forced_e[0, w] = last
-        forced_e[1, w] = first
-
-    def exchange_x(edge, column, sem):
-        for slot, r in enumerate((ty, up, down)):
-            put(forced_e.at[edge], forced_x.at[edge * 3 + slot], sem, at(r, column))
-
-    exchange_x(1, left, R_FORCED_LEFT)
-
-    @pl.when(jnp.logical_not(at_last))
-    def _():
-        exchange_x(0, right, R_FORCED_RIGHT)
-
-    exchange_y(forced_e, forced_ye, R_FORCED_YE)
-
-    @pl.when(at_first)
-    def _():
-        wait(border_land, recv_sem, R_BORDER_LAND)
-        wait(border_ice, recv_sem, R_BORDER_ICE)
-        lane = iota((ROWS, LANES), 1)
-        ocean_edge = jnp.where(lane < 4, roll_lanes(border_land[...], 4), 0.0)
-        for width in (4, 8, 16, 32, 64):
-            ocean_edge = ocean_edge + roll_lanes(ocean_edge, width)
-        melts = []
-        for w in range(ITERS):
-            melt = jnp.zeros((ROWS, LANES), F32)
-            for f in range(ICEV):
-                tile_of = jnp.concatenate([border_ice[0, w, f], border_ice[1, w, f]], axis=0)
-                here = jnp.logical_and(lane >= 4 * f, lane < 4 * f + 4)
-                melt = jnp.where(here, roll_lanes(tile_of, 4 * f + 4), melt)
-            melts.append(melt)
-        wait(border.at[pl.ds(0, n_tx)], recv_sem, R_BORDER)
-        sums = gather_edges(lambda j: border[:, j, :])
-        for w in range(ITERS):
-            edge = ocean_edge * (sums[w] + melts[w])
-            border_e[w] = edge
-            forced_x[0, w] = edge
-        for slot, r in ((1, up), (2, down)):
-            put(border_e, forced_x.at[slot], R_FORCED_RIGHT, at(r, block))
+
+    @pl.when(at_border)
+    def _():
+        meet_beside()
+        force_beside()
+
 
     wait(stat_y, recv_sem, R_STAT_Y)
     wait(stat_ye, recv_sem, R_STAT_YE)
@@ -651,14 +700,7 @@
     wait(forced_y, recv_sem, R_FORCED_Y)
     wait(forced_ye, recv_sem, R_FORCED_YE)
     wait(forced_x.at[pl.ds(3, 3)], recv_sem, R_FORCED_LEFT)
-
-    @pl.when(at_first)
-    def _():
-        wait(forced_x.at[pl.ds(1, 2)], recv_sem, R_FORCED_RIGHT)
-
-    @pl.when(jnp.logical_not(at_first))
-    def _():
-        wait(forced_x.at[pl.ds(0, 3)], recv_sem, R_FORCED_RIGHT)
+    wait(forced_x.at[pl.ds(0, 3)], recv_sem, R_FORCED_RIGHT)
 
     def forced_strips(w):
         own_edges = ((forced_e[0, w], forced_e[1, w]), (forced_ye[0, w], forced_ye[1, w]))
@@ -724,11 +766,15 @@
 
     @pl.when(at_first)
     def _():
-        wait(forced_x.at[pl.ds(0, 2)], send_sem, R_FORCED_RIGHT)
+        wait(forced_x.at[pl.ds(0, 3)], send_sem, R_FORCED_RIGHT)
 
     @pl.when(grp == 1)
     def _():
-        wait(send.at[pl.ds(0, 2)], send_sem, R_BORDER)
+        wait(send.at[0], send_sem, R_BORDER)
+
+        @pl.when(z > 0)
+        def _():
+            wait(send.at[0], send_sem, R_BORDER)
 
     @pl.when(z == half - 1)
     def _():
@@ -762,6 +808,7 @@
         pltpu.VMEM((2, ROWS, LANES), F32),
         pltpu.VMEM((2, ITERS, ROWS, LANES), F32),
         pltpu.VMEM((SLOTS, MESSAGE, LANES), F32),
+        pltpu.VMEM((1 + ITERS, ROWS, LANES), F32),
         pltpu.VMEM((2, ITERS, ICEV, 4, LANES), F32),
         pltpu.VMEM((ROWS, LANES), F32),
         pltpu.VMEM((ITERS, ROWS, LANES), F32),
@@ -769,7 +816,7 @@
         pltpu.SemaphoreType.DMA((N_LOCAL,)),
         pltpu.SemaphoreType.DMA((N_REMOTE,)),
         pltpu.SemaphoreType.DMA((N_REMOTE,)),
-        pltpu.SemaphoreType.REGULAR((GROUPS + 2,)),
+        pltpu.SemaphoreType.REGULAR((GROUPS + 4,)),
     ]
     operands = (
         innov.reshape(ITERS * PROFS * VARS, DEPTH),

time: 36.7 us -> 36.1 us (0.984)
  Pallas kernels: 35.9 us -> 35.2 us
    pallas_call x1, Pallas kernels: 35.9 us -> 35.2 us  [per_device(): pl.pallas_call(functools.partial(kernel, sizes), out_shape=jax.ShapeDtype...]
where the time goes in v4:
time: 36.1 us; the launch traced here: 35.9 us
  Pallas kernels  35.2 us (98%)
  local copies, waits for them, and re-layouts  0.67 us (2%)
    pallas_call x1, Pallas kernels, per_device(): pl.pallas_call(functools.partial(kernel, sizes), out_shape=jax.ShapeDtype...  35.2 us

profile of v4, /device:TPU:1, one launch (start us, length us, event | category | flops | bytes accessed | tf_op | source)
XLA Modules:
  0.0 35.9 jit_solution(7170703204080162555)
XLA Ops:
  0.0 35.2 %shard_map.100 = f32[5,8,8,128]{3,2,1,0:T(8,128)S(1)} custom-call(f32[512,128]{1,0:T(8,128)} %bitcast.2, f32[2,128,128]{2,1,0:T(8,128)} %weight.1, s32[2,128,128]{2,1,0:T(8,128)} %level.1, s32[2,128]{1,0:T(2,128)} %bitcast.3, s32[2,128]{1,0:T(2,128)} %cell.1, s32[8,128]{1,0:T(8,128)} %land.1, f32[8,128]{1,0:T(8,128)} %hdiff.1, f32[8,8,128]{2,1,0:T(8,128)} %vdiff.1, ...), custom_call_target="tpu_custom_call" | custom-call | tf_op jit(solution)/shard_map/pallas_call | solution.py:834
  35.2 0.7 %copy.12 = f32[5,8,8,128]{3,2,1,0:T(8,128)} copy(f32[5,8,8,128]{3,2,1,0:T(8,128)S(1)} %shard_map.100) | data formatting | bytes 327680

commit v5 on v4

--- a/solution.py
+++ b/solution.py
@@ -29,9 +29,9 @@
 
 L_LEVEL, L_WEIGHT, L_INNOV, L_TILE, L_CELL, L_LAND, L_HDIFF, L_VDIFF, L_ICE, L_COUPLING, L_OWN, L_BORDER = range(12)
 N_LOCAL = 12
-R_ROUTE, R_ICE, R_STAT_Y, R_STAT_X, R_FORCED_Y, R_FORCED_RIGHT, R_FORCED_LEFT = range(7)
-R_BORDER, R_BORDER_ICE, R_BORDER_LAND, R_STAT_YE, R_FORCED_YE = range(7, 12)
-N_REMOTE = 12
+R_ROUTE, R_ICE, R_STAT_Y, R_STAT_X, R_STAT_YE, R_BORDER, R_BORDER_ICE, R_BORDER_LAND = range(8)
+R_FORCED_Y, R_FORCED_YE, R_FORCED_RIGHT, R_FORCED_LEFT = range(8, 16, 2)
+N_REMOTE = 16
 GROUPS = 3
 S_NEAR, S_BESIDE, S_DIAGONAL = GROUPS, GROUPS + 1, GROUPS + 2
 
@@ -126,7 +126,6 @@
     rest = got - top
     y_of_row = iota((ROWS, LANES), 0).astype(F32)
     x_of_row = iota((LANES, LANES), 0).astype(F32)
-    out = []
     for w in range(ITERS):
         left, right = [], []
         for r in range(RANKS):
@@ -141,8 +140,7 @@
                         blocks.append(jnp.where(y_here, part[at : at + 1], 0.0))
                 left.append(jnp.concatenate(blocks, axis=0).astype(BF16))
                 right.append(x_here)
-        out.append(dot_nt(jnp.concatenate(left, axis=1), jnp.concatenate(right, axis=1)))
-    return out
+        yield dot_nt(jnp.concatenate(left, axis=1), jnp.concatenate(right, axis=1))
 
 
 def gather_edges(received, firsts):
@@ -154,7 +152,6 @@
     row = iota((ROWS, LANES), 0)
     y_of_row = row.astype(F32)
     zero = jnp.zeros((ROWS, LANES), F32)
-    out = []
     for w in range(ITERS):
         left, right = [], []
         for r in range(RANKS):
@@ -171,8 +168,7 @@
                 left.append(y_here)
                 right.append(jnp.concatenate(sum(blocks, []), axis=0).astype(BF16))
         sums = dot_nt(jnp.concatenate(left, axis=1).astype(BF16), jnp.concatenate(right, axis=1))
-        out.append([sums[:, i * LANES : (i + 1) * LANES] for i in range(len(firsts))])
-    return out
+        yield [sums[:, i * LANES : (i + 1) * LANES] for i in range(len(firsts))]
 
 
 def edge_ocean(ocean, first):
@@ -440,7 +436,11 @@
     def _():
         signal(barrier, (ty, tx + half, grp))
 
-    peers(z + 1, half, lambda peer: signal(barrier, (ty, peer, grp)))
+    def greet(peer):
+        signal(barrier, (ty, peer, grp))
+
+    middle = jnp.maximum(z + 1, bounds[GROUPS - 1])
+    peers(middle, half, greet)
 
     at_border = jnp.logical_and(z == 0, grp == 0)
 
@@ -481,6 +481,8 @@
         fetch(coupling, coupling_v, L_COUPLING),
     ]
 
+    peers(z + 1, middle, greet)
+
     for load in loads:
         load.wait()
     columns = [
@@ -592,9 +594,11 @@
             whole_ = (slice(None),) * (len(rows.shape) - 2)
             put(rows.at[*whole_, part], rows_y.at[*whole_, part], sem, at(r, block))
 
+    slots = ((2, down, pl.ds(4, 4)), (1, up, pl.ds(0, 4)), (0, ty, pl.ds(0, ROWS)))
+
     def exchange_x(edge, column, rows, rows_x, sem):
-        for slot, r in reversed(list(enumerate((ty, up, down)))):
-            put(rows.at[edge], rows_x.at[edge * 3 + slot], sem, at(r, column))
+        for slot, r, part in slots:
+            put(rows.at[edge, part], rows_x.at[edge * 3 + slot, part], sem, at(r, column))
 
     beside = jnp.where(grp == 0, left, right)
 
@@ -605,10 +609,10 @@
         pl.semaphore_wait(enter_sem.at[S_DIAGONAL + 1], 2)
         exchange_x(1 - grp, beside, stat_e, stat_x, R_STAT_X)
 
-    def force_beside():
+    def force_beside(w):
         @pl.when(jnp.logical_not(at_last))
         def _():
-            exchange_x(1 - grp, beside, forced_e, forced_x, R_FORCED_RIGHT + 1 - grp)
+            exchange_x(1 - grp, beside, forced_e.at[w], forced_x.at[w], R_FORCED_RIGHT + 2 * (1 - grp) + w)
 
     pl.semaphore_wait(enter_sem.at[S_DIAGONAL], 2)
     exchange_y(stat, stat_y, R_STAT_Y)
@@ -635,44 +639,46 @@
 
     own.wait()
     wait(recv.at[pl.ds(0, n_tx - 1)], recv_sem, R_ROUTE)
-    sums_e = gather_edges(lambda j: recv[:, j, :], (last_cols, first_cols))
+    window_edges = gather_edges(lambda j: recv[:, j, :], (last_cols, first_cols))
+    window_sums = gather_cells(lambda j: recv[:, j, :])
     for w in range(ITERS):
-        last, first = [oceans_e[i] * (sums_e[w][i] + melts_e[w][i]) for i in range(2)]
-        forced_e[0, w] = last
-        forced_e[1, w] = roll_lanes(first, 4)
-
-    pl.when(jnp.logical_not(at_border))(force_beside)
-    exchange_x(grp, tx * n_grp + 1 - grp, forced_e, forced_x, R_FORCED_RIGHT + grp)
-    exchange_y(forced_e, forced_ye, R_FORCED_YE)
-
-    @pl.when(at_first)
-    def _():
-        wait(border.at[tx], local_sem, L_BORDER)
-        wait(border.at[pl.ds(0, n_tx - 1)], recv_sem, R_BORDER)
-        sums_b = gather_edges(lambda j: border[:, j, :], (last_cols,))
-        for w in range(ITERS):
-            border_e[w] = border_edge[0] * (sums_b[w][0] + border_edge[1 + w])
-        for slot, r in ((1, up), (2, down), (0, ty)):
-            put(border_e, forced_x.at[slot], R_FORCED_RIGHT, (r, tx, 0))
-
-    sums = gather_cells(lambda j: recv[:, j, :])
-    for w in range(ITERS):
+        sums = next(window_edges)
+        last, first = [oceans_e[i] * (sums[i] + melts_e[w][i]) for i in range(2)]
+        forced_e[w, 0] = last
+        forced_e[w, 1] = roll_lanes(first, 4)
+        pl.when(jnp.logical_not(at_border))(functools.partial(force_beside, w))
+        exchange_x(grp, tx * n_grp + 1 - grp, forced_e.at[w], forced_x.at[w], R_FORCED_RIGHT + 2 * grp + w)
+        exchange_y(forced_e.at[w], forced_ye.at[w], R_FORCED_YE + w)
+        if w == 0:
+
+            @pl.when(at_first)
+            def _():
+                wait(border.at[tx], local_sem, L_BORDER)
+                wait(border.at[pl.ds(0, n_tx - 1)], recv_sem, R_BORDER)
+                border_sums = gather_edges(lambda j: border[:, j, :], (last_cols,))
+                for u in range(ITERS):
+                    border_e[u] = border_edge[0] * (next(border_sums)[0] + border_edge[1 + u])
+                    for slot, r, part in slots:
+                        put(border_e.at[u, part], forced_x.at[u, slot, part], R_FORCED_RIGHT + u, (r, tx, 0))
+
+        sums = next(window_sums)
         for i, (f, l) in enumerate(FORCED):
-            value = sums[w][i * ROWS : (i + 1) * ROWS] if f < VARS else None
+            value = sums[i * ROWS : (i + 1) * ROWS] if f < VARS else None
             if l == 0:
                 value = melts[w][f] if value is None else value + melts[w][f]
             forced[w * N_FORCED + i] = ocean_tile * value
-    exchange_y(forced, forced_y, R_FORCED_Y)
+        mine = pl.ds(w * N_FORCED, N_FORCED)
+        exchange_y(forced.at[mine], forced_y.at[mine], R_FORCED_Y + w)
 
     @pl.when(at_border)
     def _():
         meet_beside()
-        force_beside()
-
+        for w in range(ITERS):
+            force_beside(w)
 
     wait(stat_y, recv_sem, R_STAT_Y)
     wait(stat_ye, recv_sem, R_STAT_YE)
-    wait(stat_x, recv_sem, R_STAT_X)
+    wait(stat_x.at[pl.ds(0, 4)], recv_sem, R_STAT_X)
     own_edges = ((stat_e[0], stat_e[1]), (stat_ye[0], stat_ye[1]))
     vertical_s, diff_s, ocean_s = strips((0, 1, 2), [stat_x[i] for i in range(6)], own_edges)
     diff = (stat[LEV], stat_y[LEV])
@@ -697,14 +703,13 @@
     def vertical(l, t):
         return stat[l] if t == 0 else stat_y[l]
 
-    wait(forced_y, recv_sem, R_FORCED_Y)
-    wait(forced_ye, recv_sem, R_FORCED_YE)
-    wait(forced_x.at[pl.ds(3, 3)], recv_sem, R_FORCED_LEFT)
-    wait(forced_x.at[pl.ds(0, 3)], recv_sem, R_FORCED_RIGHT)
-
     def forced_strips(w):
-        own_edges = ((forced_e[0, w], forced_e[1, w]), (forced_ye[0, w], forced_ye[1, w]))
-        return strips(range(ICEV), [forced_x[i, w] for i in range(6)], own_edges)
+        wait(forced_y.at[pl.ds(w * N_FORCED, N_FORCED)], recv_sem, R_FORCED_Y + w)
+        wait(forced_ye.at[w], recv_sem, R_FORCED_YE + w)
+        wait(forced_x.at[w, pl.ds(0, 2)], recv_sem, R_FORCED_RIGHT + w)
+        wait(forced_x.at[w, pl.ds(3, 2)], recv_sem, R_FORCED_LEFT + w)
+        own_edges = ((forced_e[w, 0], forced_e[w, 1]), (forced_ye[w, 0], forced_ye[w, 1]))
+        return strips(range(ICEV), [forced_x[w, i] for i in range(6)], own_edges)
 
     index = {item: i for i, item in enumerate(FORCED)}
     whole = {(f, l) for f in range(F) for l in range(LEV)}
@@ -755,18 +760,19 @@
     wait(ice_v.at[0], send_sem, R_ICE)
     wait(stat, send_sem, R_STAT_Y)
     wait(stat_ye, send_sem, R_STAT_YE)
-    wait(forced_ye, send_sem, R_FORCED_YE)
-    wait(stat_x, send_sem, R_STAT_X)
-    wait(forced, send_sem, R_FORCED_Y)
-    wait(forced_x.at[pl.ds(0, 3)], send_sem, R_FORCED_LEFT)
-
-    @pl.when(jnp.logical_not(at_last))
-    def _():
-        wait(forced_x.at[pl.ds(0, 3)], send_sem, R_FORCED_RIGHT)
-
-    @pl.when(at_first)
-    def _():
-        wait(forced_x.at[pl.ds(0, 3)], send_sem, R_FORCED_RIGHT)
+    wait(stat_x.at[pl.ds(0, 4)], send_sem, R_STAT_X)
+    for w in range(ITERS):
+        wait(forced.at[pl.ds(w * N_FORCED, N_FORCED)], send_sem, R_FORCED_Y + w)
+        wait(forced_ye.at[w], send_sem, R_FORCED_YE + w)
+        wait(forced_x.at[w, pl.ds(0, 2)], send_sem, R_FORCED_LEFT + w)
+
+        @pl.when(jnp.logical_not(at_last))
+        def _():
+            wait(forced_x.at[w, pl.ds(0, 2)], send_sem, R_FORCED_RIGHT + w)
+
+        @pl.when(at_first)
+        def _():
+            wait(forced_x.at[w, pl.ds(0, 2)], send_sem, R_FORCED_RIGHT + w)
 
     @pl.when(grp == 1)
     def _():
@@ -803,10 +809,10 @@
         pltpu.VMEM((SLOTS, MESSAGE, LANES), F32),
         pltpu.VMEM((ITERS * N_FORCED, ROWS, LANES), F32),
         pltpu.VMEM((ITERS * N_FORCED, ROWS, LANES), F32),
-        pltpu.VMEM((2, ITERS, ROWS, LANES), F32),
-        pltpu.VMEM((6, ITERS, ROWS, LANES), F32),
+        pltpu.VMEM((ITERS, 2, ROWS, LANES), F32),
+        pltpu.VMEM((ITERS, 6, ROWS, LANES), F32),
         pltpu.VMEM((2, ROWS, LANES), F32),
-        pltpu.VMEM((2, ITERS, ROWS, LANES), F32),
+        pltpu.VMEM((ITERS, 2, ROWS, LANES), F32),
         pltpu.VMEM((SLOTS, MESSAGE, LANES), F32),
         pltpu.VMEM((1 + ITERS, ROWS, LANES), F32),
         pltpu.VMEM((2, ITERS, ICEV, 4, LANES), F32),

time: 36.1 us -> 36.2 us (level)
  no operation moved by 1% of the time
where the time goes in v5:
time: 36.2 us; the launch traced here: 36 us
  Pallas kernels  35.3 us (98%)
  local copies, waits for them, and re-layouts  0.67 us (2%)
    pallas_call x1, Pallas kernels, per_device(): pl.pallas_call(functools.partial(kernel, sizes), out_shape=jax.ShapeDtype...  35.3 us

profile of v5, /device:TPU:1, one launch (start us, length us, event | category | flops | bytes accessed | tf_op | source)
XLA Modules:
  0.0 36.0 jit_solution(8475711629424074004)
XLA Ops:
  0.0 35.3 %shard_map.100 = f32[5,8,8,128]{3,2,1,0:T(8,128)S(1)} custom-call(f32[512,128]{1,0:T(8,128)} %bitcast.2, f32[2,128,128]{2,1,0:T(8,128)} %weight.1, s32[2,128,128]{2,1,0:T(8,128)} %level.1, s32[2,128]{1,0:T(2,128)} %bitcast.3, s32[2,128]{1,0:T(2,128)} %cell.1, s32[8,128]{1,0:T(8,128)} %land.1, f32[8,128]{1,0:T(8,128)} %hdiff.1, f32[8,8,128]{2,1,0:T(8,128)} %vdiff.1, ...), custom_call_target="tpu_custom_call" | custom-call | tf_op jit(solution)/shard_map/pallas_call | solution.py:840
  35.4 0.7 %copy.12 = f32[5,8,8,128]{3,2,1,0:T(8,128)} copy(f32[5,8,8,128]{3,2,1,0:T(8,128)S(1)} %shard_map.100) | data formatting | bytes 327680
